TPU v7x, 128 devices: a whole 4x4x4 slice. The times are simulated.
128 devices in a mesh: tensor: 4 (over z_lo, core), expert: 32 (over y, x, z_hi).
Axes of the slice: x: 4, y: 4, z: 4 (z_hi: 2, z_lo: 2; z = z_hi * 2 + z_lo), core: 2. Of those that a mesh axis runs over, the one named last changes fastest.
Arguments:
- gate_weights: bfloat16 [32, 7168, 2048], P(None, 'expert', 'tensor'), may hold values from -0.0625 to 0.0625
- test_blocks: bfloat16 [32, 2048, 512], P('expert', 'tensor'), may hold values from -6 to 6
Outputs:
- basis: float32 [7168, 512], P('expert')
- coefficients: bfloat16 [32, 512, 2048], P('expert', None, 'tensor')
All inputs are finite; a program needn't handle non-finite values.
Results may differ from a plain program's by a relative error of at most 0.0047.
Values may be sent and summed in bfloat16 or wider, within the bound.
A program may use at most 128 MiB of HBM per device.

v0:
```python
import jax
import jax.numpy as jnp
from jax import lax
from jax.sharding import PartitionSpec as P


def local(gate_weights, test_blocks):
    owned = lax.all_to_all(gate_weights, "expert", split_axis=0, concat_axis=1, tiled=True)
    groups = lax.axis_size("expert")
    row_count = owned.shape[1] // groups
    partial_value = jnp.einsum(
        "edf,efk->dk", owned, test_blocks, preferred_element_type=jnp.float32
    )
    summed = lax.psum(partial_value, ("tensor", "expert"))
    offset = lax.axis_index("expert") * row_count
    local_sketch = lax.dynamic_slice_in_dim(summed, offset, row_count, 0)
    width = owned.shape[1]
    local_gram = jnp.dot(local_sketch.T, local_sketch, precision=lax.Precision.HIGHEST) / width
    gram = lax.psum(local_gram, "expert")
    lower = jnp.linalg.cholesky(gram)
    basis = lax.linalg.triangular_solve(
        lower, local_sketch, left_side=False, lower=True, transpose_a=True
    )
    basis_half = basis.astype(jnp.bfloat16)
    totals = jnp.einsum(
        "rk,erf->ekf",
        lax.all_gather(basis_half, "expert", axis=0, tiled=True),
        owned,
        preferred_element_type=jnp.float32,
    )
    return (basis, totals.astype(jnp.bfloat16))


def solution(mesh):
    placed = (P(None, "expert", "tensor"), P("expert", "tensor", None))
    return jax.shard_map(
        local,
        mesh=mesh,
        in_specs=placed,
        out_specs=(P("expert", None), P("expert", None, "tensor")),
        check_vma=False,
    )
```

profile of v0, /device:TPU:1, one launch (start us, length us, event | category | flops | bytes accessed | tf_op | source)
XLA Modules:
  0.0 895.4 jit_solution(3881203429283180448)
XLA Ops:
  7.2 97.1 %all_to_all.4 = bf16[32,224,512]{2,1,0:T(8,128)(2,1)S(1)} all-to-all(bf16[32,224,512]{2,1,0:T(8,128)(2,1)} %param.2), channel_id=1, replica_groups=mesh['tensor'=4,'expert'=32] {'expert'}, dimensions={0} | all-to-all | bytes 14680064 | tf_op jit(solution)/shard_map/all_to_all | solution.py:8
  104.3 3.0 copy-done.1
  107.3 7.3 fusion.2
  114.6 170.5 %all-reduce.4.cloned.1.call-done = f32[7168,512]{1,0:T(8,128)} async-done(((f32[7168,512]{1,0:T(8,128)}), f32[7168,512]{1,0:T(8,128)}) %all-reduce.4.cloned.1.call-update) | async-done | bytes 14680080 | tf_op jit(solution)/shard_map/psum | solution.py:14
  285.2 3.2 convolution_multiply_fusion
  288.4 0.2 all-gather.2.cloned.1.call-start
  288.7 328.6 %all-reduce.6.cloned.1.call-done = f32[512,512]{0,1:T(8,128)} async-done(((f32[512,512]{0,1:T(8,128)}), f32[512,512]{0,1:T(8,128)}) %all-reduce.6.cloned.1.call-update) | async-done | bytes 1048592 | tf_op jit(solution)/shard_map/psum | solution.py:19
  617.3 1.6 copy.5
  618.8 1.4 fusion.1
  620.3 11.7 %cholesky.104 = f32[128,128]{1,0:T(8,128)S(1)} custom-call(f32[128,128]{1,0:T(8,128)S(1)} %cholesky.266), custom_call_target="Cholesky" | custom-call | tf_op jit(solution)/shard_map/jit(cholesky)/cholesky | solution.py:20
  632.0 0.1 cholesky.224
  632.2 9.8 %custom-call.30 = f32[1,128,128]{1,2,0:T(8,128)S(1)} custom-call(f32[1,128,128]{2,1,0:T(8,128)S(1)} %get-tuple-element.31), custom_call_target="InvertDiagBlocksLowerTriangular" | custom-call | tf_op jit(solution)/shard_map/jit(cholesky)/cholesky | solution.py:20
  642.0 0.3 constant_dynamic-update-slice_fusion.3
  642.3 0.3 convolution_subtract_fusion
  642.7 11.7 %cholesky.217 = f32[128,128]{1,0:T(8,128)S(1)} custom-call(f32[128,128]{1,0:T(8,128)S(1)} %cholesky.270), custom_call_target="Cholesky" | custom-call | tf_op jit(solution)/shard_map/jit(cholesky)/cholesky | solution.py:20
  654.4 10.0 %custom-call.31 = f32[1,128,128]{1,2,0:T(8,128)S(1)} custom-call(f32[1,128,128]{2,1,0:T(8,128)S(1)} %get-tuple-element.28), custom_call_target="InvertDiagBlocksLowerTriangular" | custom-call | tf_op jit(solution)/shard_map/jit(cholesky)/cholesky | solution.py:20
  664.4 0.3 convolution_dynamic-update-slice_fusion
  664.7 0.4 convolution_subtract_fusion.1
  665.1 11.7 %cholesky.238 = f32[128,128]{1,0:T(8,128)S(1)} custom-call(f32[128,128]{1,0:T(8,128)S(1)} %cholesky.275), custom_call_target="Cholesky" | custom-call | tf_op jit(solution)/shard_map/jit(cholesky)/cholesky | solution.py:20
  676.8 9.8 %custom-call.32 = f32[1,128,128]{1,2,0:T(8,128)S(1)} custom-call(f32[1,128,128]{2,1,0:T(8,128)S(1)} %get-tuple-element.25), custom_call_target="InvertDiagBlocksLowerTriangular" | custom-call | tf_op jit(solution)/shard_map/jit(cholesky)/cholesky | solution.py:20
  686.6 0.2 convolution_dynamic-update-slice_fusion.1
  686.9 0.4 convolution_subtract_fusion.5
  687.2 11.7 %cholesky.255 = f32[128,128]{1,0:T(8,128)S(1)} custom-call(f32[128,128]{1,0:T(8,128)S(1)} %convolution_subtract_fusion.5), custom_call_target="Cholesky" | custom-call | tf_op jit(solution)/shard_map/jit(cholesky)/cholesky | solution.py:20
  699.0 0.7 compare_reduce_fusion.1
  699.7 0.7 compare_reduce_fusion
  700.4 0.6 compare_reduce_fusion.2
  703.7 0.4 select_select_fusion
  704.1 8.2 while.1
  704.1 0.1 constant_dynamic-slice_fusion.2
  704.2 0.6 fusion.47
  704.7 1.4 bitcast_dynamic-update-slice_fusion.2
  706.2 0.6 fusion.47
  706.8 1.4 bitcast_dynamic-update-slice_fusion.2
  708.2 0.6 fusion.47
  708.8 1.4 bitcast_dynamic-update-slice_fusion.2
  710.3 0.6 fusion.47
  710.9 1.4 bitcast_dynamic-update-slice_fusion.2
  712.3 39.3 %custom-call.33 = f32[4,128,128]{1,2,0:T(8,128)S(1)} custom-call(f32[4,128,128]{2,1,0:T(8,128)S(1)} %get-tuple-element.9), custom_call_target="InvertDiagBlocksLowerTriangular" | custom-call | tf_op jit(solution)/shard_map/triangular_solve | solution.py:21
  751.6 1.1 fusion.21
  752.7 1.2 convolution_subtract_fusion.2
  753.9 0.2 fusion.25
  754.2 1.3 convolution_subtract_fusion.3
  755.4 0.2 fusion.24
  755.7 1.4 convolution_subtract_fusion.4
  757.1 0.2 fusion.23
  757.3 0.9 fusion.36
  758.2 120.7 %all-gather.2.cloned.1.call-done = bf16[7168,512]{1,0:T(8,128)(2,1)} async-done(((bf16[224,512]{1,0:T(8,128)(2,1)}), bf16[7168,512]{1,0:T(8,128)(2,1)}) %all-gather.2.cloned.1.call-update) | async-done | bytes 7340048 | tf_op jit(solution)/shard_map/all_gather | solution.py:27
  879.0 9.9 %fusion = bf16[1,512,512]{2,1,0:T(8,128)(2,1)} fusion(bf16[7168,512]{1,0:T(8,128)(2,1)} %all-gather.2.cloned.1.call-done, bf16[7168,512]{1,0:T(8,128)(2,1)} %bitcast.62), kind=kOutput, calls=%fused_computation.4 | convolution fusion | flops 3758358528 | bytes 15204352 | tf_op jit(solution)/shard_map/rk,erf->ekf/dot_general | solution.py:25
  (21 shorter events, 0.5 us)
Async XLA Ops:
  7.2 100.1 %copy-start = (bf16[1,512,512]{2,1,0:T(8,128)(2,1)S(1)}, bf16[1,512,512]{2,1,0:T(8,128)(2,1)}, u32[]{:S(2)}) copy-start(bf16[1,512,512]{2,1,0:T(8,128)(2,1)} %param.3) | copy-start | bytes 1572868
  7.2 278.0 %all-reduce.4.cloned.1.call-start = ((), (), s32[]{:S(2)}) async-start(), calls=%async_computation.1 | async-start | bytes 29360128 | tf_op jit(solution)/shard_map/psum | solution.py:14
  104.3 3.0 copy-start.1
  114.6 502.7 %all-reduce.6.cloned.1.call-start = ((), (), s32[]{:S(2)}) async-start(), calls=%async_computation.2 | async-start | bytes 2097152 | tf_op jit(solution)/shard_map/psum | solution.py:19
  288.4 590.6 %all-gather.2.cloned.1.call-start = ((), (), s32[]{:S(2)}) async-start(), calls=%async_computation.3 | async-start | bytes 7569408 | tf_op jit(solution)/shard_map/all_gather | solution.py:27
Sparse Core Ops, SparseCore 0:
  114.7 170.4 all-reduce.3
  288.5 328.6 all-reduce.5
  758.4 120.5 all-gather.1
where the time goes:
time: 896 us; the launch traced here: 895 us
  waiting for transfers between devices  620 us (69%)
  other arithmetic  121 us (14%)
  blocking collectives  97.1 us (11%)
  matrix products  28 us (3%)
  between operations  16.6 us (2%)
  local copies, waits for them, and re-layouts  12.8 us (1%)
    psum x1, waiting for transfers between devices, local(): gram = lax.psum(local_gram, 'expert')  329 us
    psum x1, waiting for transfers between devices, local(): summed = lax.psum(partial_value, ('tensor', 'expert'))  171 us
    all_gather x1, waiting for transfers between devices, local(): lax.all_gather(basis_half, 'expert', axis=0, tiled=True)  121 us
    all_to_all x1, blocking collectives, local(): lax.all_to_all(gate_weights, 'expert', split_axis=0, concat_axis=1, tiled...  97.1 us
    another operation x14, other arithmetic, local(): lower = jnp.linalg.cholesky(gram)  78.7 us
    another operation x3, other arithmetic, local(): lax.linalg.triangular_solve(lower, local_sketch, left_side=False, lower=T...  39.7 us
  transfers between devices with their start and end apart: 3, of which 3 were waited for; matrix products, arithmetic and copies ran while one was open for 0% of the time, Pallas kernels for 0%

commit v1 on v0

v1 whole, which is shorter than its diff:
```python
import functools

import jax
import jax.numpy as jnp
from jax import lax
from jax.experimental import pallas as pl
from jax.experimental.pallas import tpu as pltpu
from jax.sharding import PartitionSpec as P

MESH = pl.DeviceIdType.MESH
F32, BF16 = jnp.float32, jnp.bfloat16
SIDE = 4
CHIP_ROWS = 112
HALF = 256
PARTS = ((0, 32, "xyz"), (32, 16, "yzx"), (48, 16, "zxy"), (64, 16, "xyz"), (80, 16, "yzx"), (96, 16, "zxy"))
BATCHES = ((1, 2, 0), (4, 5, 3))
ALL = sum(BATCHES, ())


def where():
    t, e = lax.axis_index("tensor"), lax.axis_index("expert")
    return {"y": e // 8, "x": (e // 2) % 4, "z": (e % 2) * 2 + t // 2, "c": t % 2}


def device(at):
    return (at["z"] % 2) * 2 + at["c"], (at["y"] * 4 + at["x"]) * 2 + at["z"] // 2


def moved(at, axis, by):
    return {**at, axis: lax.rem(at[axis] + by, 2 if axis == "c" else SIDE)}


def send(src, dst, sems, index, at):
    copy = pltpu.make_async_remote_copy(
        src_ref=src, dst_ref=dst, send_sem=sems[0].at[index], recv_sem=sems[1].at[index],
        device_id=device(at), device_id_type=MESH,
    )
    copy.start()
    return copy


def cut(ref, fixed, rows=None, lead=(), dims="yxz", extra=()):
    tail = () if rows is None else (*extra, rows)
    return ref.at[(*lead, *(fixed.get(d, slice(None)) for d in dims), *tail)]


def sum_kernel(g_hbm, t_ref, acc, own_rows, *rest):
    count = len(PARTS)

    def take(n):
        nonlocal rest
        taken, rest = rest[:n], rest[n:]
        return taken

    g, f_ref = take(2)
    turned1, turned2 = take(count), take(count)
    away, landed, q = take(count), take(count), take(count)
    stage1, sums1, stage2, sums2, stage3 = (take(count) for _ in range(5))
    (local_sem,) = take(1)
    turn_sems, core_sems, rs_sems, ag_sems, pair_sems = (take(2) for _ in range(5))
    me = where()
    c = me["c"]
    twin = moved(me, "c", 1)
    peers = [twin] + [moved(me, a, k) for a in "xyz" for k in (1, 2, 3)]
    barrier = pltpu.get_barrier_semaphore()
    for peer in peers:
        pl.semaphore_signal(barrier, inc=1, device_id=device(peer), device_id_type=MESH)
    pl.semaphore_wait(barrier, len(peers))
    sent = []

    def turn(p, step):
        first, rows, order = PARTS[p]
        axis, at = order[step], pl.ds(first, rows)
        either = (slice(None),)
        place = lambda spot: {axis: spot[axis] // 2 if axis == "z" else spot[axis]}
        source = lambda fixed: cut(g_hbm, fixed, at, extra=either) if step == 0 else cut((turned1, turned2)[step - 1][p], fixed)
        target = lambda fixed: cut(g, fixed, at, extra=either) if step == 2 else cut((turned1, turned2)[step][p], fixed)
        kept = pltpu.make_async_copy(source(place(me)), target(place(me)), local_sem.at[p * 3 + step])
        kept.start()
        started = []
        for k in (2,) if axis == "z" else (2, 1, 3):
            peer = moved(me, axis, k)
            started.append(send(source(place(peer)), target(place(me)), turn_sems, p * 9 + step * 3 + k - 1, peer))
        sent.extend(started)
        return kept, started

    def turned(copies):
        copies[0].wait()
        for copy in copies[1]:
            copy.wait_recv()

    moves = {p: turn(p, 0) for p in ALL}
    for step in (1, 2):
        for p in ALL:
            turned(moves[p])
            moves[p] = turn(p, step)

    def product(p, y, column):
        first, rows, _ = PARTS[p]
        left = g[y, :, :, :, pl.ds(first, rows)].reshape(16 * rows, 512)
        right = t_ref[:, pl.ds(pl.multiple_of(column * HALF, HALF), HALF)]
        return jnp.dot(left, right, preferred_element_type=F32).reshape(SIDE, SIDE, rows, HALF)

    def pair(p):
        @pl.loop(0, SIDE)
        def _(y):
            away[p][y] = product(p, y, 1 - c).astype(BF16)

        copy = send(away[p], landed[p], core_sems, p, twin)
        sent.append(copy)
        return copy

    def both(p, copy):
        copy.wait_recv()

        @pl.loop(0, SIDE)
        def _(y):
            q[p][y] = (product(p, y, c) + landed[p][y].astype(F32)).astype(BF16)

    sources, slots, totals = (q, sums1, sums2), (stage1, stage2, stage3), (sums1, sums2)

    def left_after(p, step):
        return "".join(d for d in "yxz" if d not in PARTS[p][2][:step])

    def scatter(p, step):
        axis, started = PARTS[p][2][step], []
        for k in (2, 1, 3):
            peer = moved(me, axis, k)
            source = cut(sources[step][p], {axis: peer[axis]}, dims=left_after(p, step))
            started.append(send(source, slots[step][p].at[k - 1], rs_sems, p * 9 + step * 3 + k - 1, peer))
        sent.extend(started)
        return started

    def add(p, step, started):
        first, rows, order = PARTS[p]
        axis = order[step]
        for copy in started:
            copy.wait_recv()
        mine = cut(sources[step][p], {axis: me[axis]}, dims=left_after(p, step))

        def total(at):
            value = mine[(*at,)].astype(F32)
            for k in range(3):
                value += slots[step][p][(k, *at)].astype(F32)
            return value

        if step == 0:
            @pl.loop(0, SIDE)
            def _(a):
                totals[0][p][a] = total((a,))
        elif step == 1:
            totals[1][p][...] = total((slice(None),))
        else:
            f_ref[c, me["y"], me["x"], me["z"], pl.ds(first, rows)] = total((slice(None),)).astype(BF16)

    def gather(p, step):
        first, rows, order = PARTS[p]
        part = cut(f_ref, {a: me[a] for a in order[:step + 1]}, pl.ds(first, rows), (c,))
        started = [
            send(part, part, ag_sems, p * 9 + step * 3 + k - 1, moved(me, order[step], k)) for k in (2, 1, 3)
        ]
        sent.extend(started)
        return started

    def share(p, k):
        first, rows, order = PARTS[p]
        axis = order[0]
        part = cut(f_ref, {axis: lax.rem(me[axis] + SIDE - k, SIDE)}, pl.ds(first, rows), (c,))
        copy = send(part, part, pair_sems, p * SIDE + k, twin)
        sent.append(copy)
        return copy

    pairs = {}
    for batch in BATCHES:
        for p in batch:
            turned(moves[p])
            pairs[p] = pair(p)
        for p in batch:
            both(p, pairs[p])
            moves[p] = scatter(p, 0)
    for step in range(3):
        for batch in BATCHES:
            for p in batch:
                add(p, step, moves[p])
                moves[p] = scatter(p, step + 1) if step < 2 else gather(p, 2)
    for step in (1, 0):
        for batch in BATCHES:
            for p in batch:
                for copy in moves[p]:
                    copy.wait_recv()
                moves[p] = gather(p, step)
                if step == 0:
                    pairs[p] = [share(p, 0)]
    for batch in BATCHES:
        for p in batch:
            for copy, k in zip(moves[p], (2, 1, 3)):
                copy.wait_recv()
                pairs[p].append(share(p, k))
    acc[...] = jnp.zeros_like(acc)
    for batch in BATCHES:
        for p in batch:
            for copy in pairs[p]:
                copy.wait_recv()
            first, rows, _ = PARTS[p]

            @pl.loop(0, SIDE)
            def _(y):
                at = pl.ds(first, rows)
                s = jnp.concatenate([f_ref[h, y, :, :, at].reshape(16 * rows, HALF) for h in (0, 1)], axis=1)
                w = g[y, :, :, :, at].reshape(16 * rows, 512)
                acc[...] += lax.dot_general(
                    s, jnp.concatenate([s, w], axis=1), (((0,), (0,)), ((), ())), preferred_element_type=F32
                )

    for h in (0, 1):
        own_rows[h] = f_ref[h, me["y"], me["x"], pl.ds(me["z"] // 2 * 2, 2)]
    for copy in sent:
        copy.wait_send()


def finish_kernel(acc, own, basis_ref, c_ref, ok_ref):
    k = acc.shape[0]
    row = lax.broadcasted_iota(jnp.int32, (k, k), 0)
    col = lax.broadcasted_iota(jnp.int32, (k, k), 1)
    eye = (row == col).astype(F32)
    gram = acc[:, :k] / 7168
    diagonal = gram * eye
    down = lax.rsqrt(jnp.sum(diagonal, axis=1, keepdims=True))
    across = lax.rsqrt(jnp.sum(diagonal, axis=0, keepdims=True))
    a = gram * down * across

    def dot(u, v, across=False):
        return lax.dot_general(u, v, (((1,), (1 if across else 0,)), ((), ())), preferred_element_type=F32)

    def halves(u):
        high = u.astype(BF16)
        return high, (u - high.astype(F32)).astype(BF16)

    def fine(u, v, across=False):
        (uh, ul), (vh, vl) = halves(u), halves(v)
        return dot(uh, vh, across) + (dot(uh, vl, across) + dot(ul, vh, across))

    def coarse(u, v, across=False):
        return dot(u.astype(BF16), v.astype(BF16), across)

    half_lower = jnp.where(row > col, 1.0, 0.5 * eye)

    def gap(x, mul):
        return mul(mul(x, a), x, True) - eye

    def better(x, e, mul):
        phi = e * half_lower
        y = mul(phi, x)
        return x - (y - mul(phi, y))

    phi = (a - eye) * half_lower
    x = eye - (phi - coarse(phi, phi))
    x = better(x, gap(x, coarse), coarse)
    x = better(x, gap(x, fine), fine)
    left = gap(x, fine)
    ok_ref[0, 0] = jnp.sum(left * left)
    x = x * across
    c_ref[...] = fine(x, acc[:, k:]).astype(BF16)
    high, low = halves(x)
    rows = jnp.concatenate([own[0], own[1]], axis=1)
    basis_ref[...] = dot(rows, high, True) + dot(rows, low, True)


def local(gate_weights, test_blocks):
    weights = gate_weights.reshape(SIDE, SIDE, 2, 2, CHIP_ROWS, 512)
    spread = lambda step, rows: tuple(SIDE for _ in range(3 - step)) + (rows, HALF)
    sizes = [rows for _, rows, _ in PARTS]
    scratch = [
        pltpu.VMEM((SIDE, SIDE, 2, 2, CHIP_ROWS, 512), BF16),
        pltpu.VMEM((2, SIDE, SIDE, SIDE, CHIP_ROWS, HALF), BF16),
    ]
    scratch += [pltpu.VMEM((SIDE, SIDE, 2, 2, rows, 512), BF16) for rows in sizes * 2]
    scratch += [pltpu.VMEM(spread(0, rows), BF16) for rows in sizes * 3]
    for step, kind in ((1, BF16), (2, F32), (3, F32)):
        scratch += [pltpu.VMEM((3,) + spread(step, rows), kind) for rows in sizes]
        if step < 3:
            scratch += [pltpu.VMEM(spread(step, rows), F32) for rows in sizes]
    n = len(PARTS)
    scratch += [pltpu.SemaphoreType.DMA((3 * n,))]
    for size in (9, 1, 9, 9, 4):
        scratch += [pltpu.SemaphoreType.DMA((size * n,))] * 2
    vmem, hbm = pl.BlockSpec(memory_space=pltpu.VMEM), pl.BlockSpec(memory_space=pl.ANY)
    acc, rows = pl.pallas_call(
        sum_kernel,
        out_shape=(
            jax.ShapeDtypeStruct((512, 1024), F32),
            jax.ShapeDtypeStruct((2, 2, CHIP_ROWS, HALF), BF16),
        ),
        in_specs=[hbm, vmem],
        out_specs=(vmem, vmem),
        scratch_shapes=scratch,
        compiler_params=pltpu.CompilerParams(collective_id=0, has_side_effects=True, vmem_limit_bytes=60 << 20),
    )(weights, test_blocks[0])
    rows = rows.reshape(2, 224, HALF)
    basis, coefficients, gap = pl.pallas_call(
        finish_kernel,
        out_shape=(
            jax.ShapeDtypeStruct((224, 512), F32),
            jax.ShapeDtypeStruct((512, 512), BF16),
            jax.ShapeDtypeStruct((1, 1), F32),
        ),
        in_specs=[vmem, vmem],
        out_specs=(vmem, vmem, pl.BlockSpec(memory_space=pltpu.SMEM)),
        compiler_params=pltpu.CompilerParams(vmem_limit_bytes=60 << 20),
    )(acc, rows)

    def exact():
        lower = jnp.linalg.cholesky(acc[:, :512] / 7168)
        x = lax.linalg.triangular_solve(lower, jnp.eye(512, dtype=F32), left_side=True, lower=True)
        high = functools.partial(jnp.dot, precision=lax.Precision.HIGHEST)
        s = jnp.concatenate([rows[0], rows[1]], axis=1).astype(F32)
        return high(s, x.T), high(x, acc[:, 512:]).astype(BF16)

    basis, coefficients = lax.cond(gap[0, 0] < 1e-4, lambda: (basis, coefficients), exact)
    return basis, coefficients[None]


def solution(mesh):
    placed = (P(None, "expert", "tensor"), P("expert", "tensor", None))
    return jax.shard_map(
        local,
        mesh=mesh,
        in_specs=placed,
        out_specs=(P("expert", None), P("expert", None, "tensor")),
        check_vma=False,
    )
```

time: 896 us -> 343 us (0.38)
  waiting for transfers between devices: 620 us -> 0 us
  Pallas kernels: 0 us -> 170 us
  blocking collectives: 97.1 us -> 0 us
  between operations: 16.6 us -> 2.67 us
  matrix products: 28 us -> 17 us
    psum x2 -> x0, waiting for transfers between devices: 499 us -> none  [the longest x1 329 us: local(): gram = lax.psum(local_gram, 'expert')]
    pallas_call x0 -> x2, Pallas kernels: none -> 170 us  [the longest x1 161 us: local(): pl.pallas_call(sum_kernel, out_shape=(jax.ShapeDtypeStruct((512, 1024), F...]
    all_gather x1 -> x0, waiting for transfers between devices: 121 us -> none  [local(): lax.all_gather(basis_half, 'expert', axis=0, tiled=True)]
    all_to_all x1 -> x0, blocking collectives: 97.1 us -> none  [local(): lax.all_to_all(gate_weights, 'expert', split_axis=0, concat_axis=1, tiled...]
    dot_general x3 -> x2, matrix products: 20.4 us -> 4.15 us  [exact(): return (high(s, x.T), high(x, acc[:, 512:]).astype(BF16))]
  transfers between devices with their start and end apart: 3 -> 0, of which waited for: 3 -> 0; matrix products, arithmetic and copies ran while one was open for 0% -> 0% of each run, Pallas kernels for 0% -> 0%
where the time goes in v1:
time: 343 us; the launch traced here: 337 us
  Pallas kernels  170 us (50%)
  other arithmetic  125 us (36%)
  local copies, waits for them, and re-layouts  19 us (6%)
  matrix products  17 us (5%)
  loops' own time  3.46 us (1%)
    pallas_call x1, Pallas kernels, local(): pl.pallas_call(sum_kernel, out_shape=(jax.ShapeDtypeStruct((512, 1024), F...  161 us
    another operation x14, other arithmetic, exact(): lower = jnp.linalg.cholesky(acc[:, :512] / 7168)  83.1 us
    another operation x3, other arithmetic, exact(): lax.linalg.triangular_solve(lower, jnp.eye(512, dtype=F32), left_side=Tru...  40.4 us
    another operation x13, local copies, waits for them, and re-layouts  13.7 us
    pallas_call x1, Pallas kernels, local(): pl.pallas_call(finish_kernel, out_shape=(jax.ShapeDtypeStruct((224, 512),...  8.83 us
    another operation x6, matrix products, exact(): lower = jnp.linalg.cholesky(acc[:, :512] / 7168)  7.2 us

profile of v1, /device:TPU:1, one launch (start us, length us, event | category | flops | bytes accessed | tf_op | source)
XLA Modules:
  0.0 337.4 jit_solution(719166689225338235)
XLA Ops:
  0.6 161.3 %shard_map.45 = (f32[512,1024]{1,0:T(8,128)S(1)}, bf16[2,2,112,256]{3,2,1,0:T(8,128)(2,1)S(1)}) custom-call(bf16[4,4,2,2,112,512]{5,4,3,2,1,0:T(8,128)(2,1)} %bitcast.59, bf16[512,512]{1,0:T(8,128)(2,1)} %bitcast.62), custom_call_target="tpu_custom_call" | custom-call | tf_op jit(solution)/shard_map/pallas_call | solution.py:288
  162.0 8.8 %shard_map.46 = (f32[224,512]{1,0:T(8,128)}, bf16[512,512]{1,0:T(8,128)(2,1)}, f32[1,1]{1,0:T(1,128)}) custom-call(f32[512,1024]{1,0:T(8,128)S(1)} %get-tuple-element.22.acc, bf16[2,224,256]{2,1,0:T(8,128)(2,1)S(1)} %bitcast.60), custom_call_target="tpu_custom_call" | custom-call | tf_op jit(solution)/shard_map/pallas_call | solution.py:300
  171.5 164.6 %conditional.1 = (f32[224,512]{1,0:T(8,128)}, bf16[1,512,512]{2,1,0:T(8,128)(2,1)}) conditional(s32[]{:T(128)} %bitcast.18, (bf16[2,224,256]{2,1,0:T(8,128)(2,1)S(1)}, f32[512,1024]{1,0:T(8,128)S(1)}) %tuple.53, (bf16[512,512]{1,0:T(8,128)(2,1)}, f32[224,512]{1,0:T(8,128)}) %tuple.52), branch_computations={%region_0.9_spmd, %region_9.10_spmd} | conditional | flops 3730833920 | bytes 43946320 | solution.py:319
  171.5 1.3 copy-done
  172.9 2.1 copy.9
  175.0 1.1 slice_multiply_fusion
  176.1 1.6 copy.8
  177.6 0.2 fusion.2
  177.9 1.0 copy-done.1
  178.9 11.7 %cholesky.5 = f32[128,128]{1,0:T(8,128)S(1)} custom-call(f32[128,128]{1,0:T(8,128)S(1)} %cholesky.100), custom_call_target="Cholesky" | custom-call | tf_op jit(solution)/shard_map/cond/branch_0_fun/jit(cholesky)/cholesky | solution.py:313
  190.6 9.8 %custom-call.26 = f32[1,128,128]{1,2,0:T(8,128)S(1)} custom-call(f32[1,128,128]{2,1,0:T(8,128)S(1)} %get-tuple-element.60), custom_call_target="InvertDiagBlocksLowerTriangular" | custom-call | tf_op jit(solution)/shard_map/cond/branch_0_fun/jit(cholesky)/cholesky | solution.py:313
  200.6 1.2 constant_dynamic-update-slice_fusion.3
  201.8 1.3 convolution_subtract_fusion.3
  203.1 0.7 copy-done.2
  203.8 11.7 %cholesky.29 = f32[128,128]{1,0:T(8,128)S(1)} custom-call(f32[128,128]{1,0:T(8,128)S(1)} %cholesky.104), custom_call_target="Cholesky" | custom-call | tf_op jit(solution)/shard_map/cond/branch_0_fun/jit(cholesky)/cholesky | solution.py:313
  215.5 0.7 compare_reduce_fusion.2
  217.5 10.0 %custom-call.27 = f32[1,128,128]{1,2,0:T(8,128)S(1)} custom-call(f32[1,128,128]{2,1,0:T(8,128)S(1)} %get-tuple-element.57), custom_call_target="InvertDiagBlocksLowerTriangular" | custom-call | tf_op jit(solution)/shard_map/cond/branch_0_fun/jit(cholesky)/cholesky | solution.py:313
  227.5 1.2 convolution_dynamic-update-slice_fusion
  228.7 1.3 convolution_subtract_fusion.4
  230.0 0.6 cholesky.111
  230.6 13.2 %cholesky.62 = f32[128,128]{1,0:T(8,128)} custom-call(f32[128,128]{1,0:T(8,128)} %cholesky.111), custom_call_target="Cholesky" | custom-call | tf_op jit(solution)/shard_map/cond/branch_0_fun/jit(cholesky)/cholesky | solution.py:313
  243.7 1.5 select_reduce_fusion.1
  245.2 0.7 compare_reduce_fusion.1
  246.6 11.3 %custom-call.28 = f32[1,128,128]{1,2,0:T(8,128)} custom-call(f32[1,128,128]{2,1,0:T(8,128)} %get-tuple-element.54), custom_call_target="InvertDiagBlocksLowerTriangular" | custom-call | tf_op jit(solution)/shard_map/cond/branch_0_fun/jit(cholesky)/cholesky | solution.py:313
  257.9 1.0 convolution_dynamic-update-slice_fusion.1
  258.9 1.2 convolution_subtract_fusion.5
  260.2 11.7 %cholesky.89 = f32[128,128]{1,0:T(8,128)S(1)} custom-call(f32[128,128]{1,0:T(8,128)S(1)} %convolution_subtract_fusion.5), custom_call_target="Cholesky" | custom-call | tf_op jit(solution)/shard_map/cond/branch_0_fun/jit(cholesky)/cholesky | solution.py:313
  272.2 0.7 compare_reduce_fusion
  273.6 1.1 select_select_fusion
  274.7 11.7 %while.1 = (s32[]{:T(128)}, f32[512,512]{1,0:T(8,128)}, s32[4,2]{0,1:T(2,128)S(1)}, f32[4,128,128]{2,1,0:T(8,128)S(1)}, s32[]{:T(128)}) while((s32[]{:T(128)}, f32[512,512]{1,0:T(8,128)}, s32[4,2]{0,1:T(2,128)S(1)}, f32[4,128,128]{2,1,0:T(8,128)S(1)}, s32[]{:T(128)}) %tuple.47), condition=%wide.while_cond, body=%wide.while_body.sunk | while | flops 2 | bytes 131181 | solution.py:314
  274.8 0.6 fusion.47
  275.4 2.3 bitcast_dynamic-update-slice_fusion.2
  277.7 0.6 fusion.47
  278.3 2.3 bitcast_dynamic-update-slice_fusion.2
  280.7 0.6 fusion.47
  281.3 2.3 bitcast_dynamic-update-slice_fusion.2
  283.6 0.6 fusion.47
  284.2 2.2 bitcast_dynamic-update-slice_fusion.2
  286.4 39.3 %custom-call.29 = f32[4,128,128]{1,2,0:T(8,128)S(1)} custom-call(f32[4,128,128]{2,1,0:T(8,128)S(1)} %get-tuple-element.36), custom_call_target="InvertDiagBlocksLowerTriangular" | custom-call | tf_op jit(solution)/shard_map/cond/branch_0_fun/triangular_solve | solution.py:314
  325.8 0.3 fusion.14
  326.3 1.2 convolution_subtract_fusion.1
  327.5 0.4 fusion.29
  327.9 1.3 convolution_subtract_fusion
  329.2 0.4 fusion.27
  329.7 1.6 convolution_subtract_fusion.2
  331.2 0.4 fusion.26
  331.7 2.7 fusion
  334.3 1.5 fusion.8
  (19 shorter events, 0.8 us)
Async XLA Ops:
  171.5 1.4 copy-start
  177.9 1.0 copy-start.1
  203.1 0.7 copy-start.2

commit v2 on v0

v2 whole, which is shorter than its diff:
```python
import functools

import jax
import jax.numpy as jnp
from jax import lax
from jax.experimental import pallas as pl
from jax.experimental.pallas import tpu as pltpu
from jax.sharding import PartitionSpec as P

MESH = pl.DeviceIdType.MESH
F32, BF16 = jnp.float32, jnp.bfloat16
SIDE = 4
CHIP_ROWS = 112
HALF = 256
VMEM_LIMIT = 62 << 20
ROWS = 16
ORDERS = ("xyz", "yzx", "zxy", "xyz", "yzx", "zxy", "xyz")
AROUND = (0, 1, 5, 6)
PASSED = (0, 1, 3, 4)
TURN_ORDERS = ("xyz", "yzx", "zxy")
PLAN = (
    ("turn", 0, 0), ("turn", 1, 0), ("turn", 2, 0), ("turn", 3, 0), ("turn", 4, 0), ("turn", 5, 0), ("turn", 6, 0),
    ("turn", 7, 0), ("turn", 8, 0), ("turn", 9, 0), ("turn", 10, 0), ("turn", 11, 0), ("turn", 12, 0),
    ("turn", 13, 0), ("turn", 1, 1), ("turn", 2, 1), ("turn", 0, 1), ("turn", 4, 1), ("turn", 5, 1), ("turn", 3, 1),
    ("turn", 7, 1), ("turn", 8, 1), ("turn", 6, 1), ("turn", 10, 1), ("turn", 11, 1), ("turn", 9, 1), ("turn", 13, 1),
    ("turn", 1, 2), ("turn", 12, 1), ("turn", 0, 2), ("turn", 4, 2), ("turn", 2, 2), ("turn", 3, 2), ("turn", 7, 2),
    ("turn", 5, 2), ("turn", 6, 2), ("turn", 10, 2), ("turn", 8, 2), ("turn", 9, 2), ("turn", 13, 2), ("turn", 11, 2),
    ("pair", 0), ("both", 0), ("turn", 12, 2), ("pair", 1), ("both", 1), ("pair", 2), ("pair", 3), ("both", 2),
    ("both", 3), ("pair", 4), ("both", 4), ("pair", 5), ("pair", 6), ("onward", 0), ("onward", 1), ("both", 5),
    ("both", 6), ("add", 2, 0), ("add", 3, 0), ("add", 4, 0), ("onward", 5), ("add", 0, 0), ("add", 1, 0),
    ("onward", 6), ("add", 4, 1), ("add", 3, 1), ("add", 2, 1), ("add", 5, 0), ("add", 0, 1), ("add", 6, 0),
    ("add", 2, 2), ("add", 4, 2), ("add", 1, 1), ("add", 3, 2), ("add", 0, 2), ("add", 5, 1), ("further", 4, 1),
    ("further", 3, 1), ("add", 1, 2), ("add", 6, 1), ("further", 0, 1), ("further", 2, 1), ("add", 5, 2),
    ("further", 1, 1), ("further", 4, 0), ("further", 3, 0), ("add", 6, 2), ("further", 2, 0), ("further", 0, 0),
    ("further", 5, 1), ("further", 1, 0), ("further", 6, 1), ("forward", 4), ("forward", 3), ("forward", 1),
    ("forward", 0), ("share_rest", 2), ("further", 6, 0), ("further", 5, 0), ("share_rest", 4), ("share_rest", 3),
    ("share_rest", 1), ("share_rest", 0), ("multiply", 2), ("multiply", 3), ("multiply", 0), ("multiply", 1),
    ("share_rest", 5), ("share_rest", 6), ("multiply", 4), ("multiply", 5), ("multiply", 6),
)


def where():
    t, e = lax.axis_index("tensor"), lax.axis_index("expert")
    return {"y": e // 8, "x": (e // 2) % 4, "z": (e % 2) * 2 + t // 2, "c": t % 2}


def device(at):
    return (at["z"] % 2) * 2 + at["c"], (at["y"] * 4 + at["x"]) * 2 + at["z"] // 2


def moved(at, axis, by):
    return {**at, axis: lax.rem(at[axis] + by, 2 if axis == "c" else SIDE)}


def send(src, dst, sems, index, at):
    copy = pltpu.make_async_remote_copy(
        src_ref=src, dst_ref=dst, send_sem=sems[0].at[index], recv_sem=sems[1].at[index],
        device_id=device(at), device_id_type=MESH,
    )
    copy.start()
    return copy


def cut(ref, fixed, rows=None, lead=(), dims="yxz", extra=()):
    tail = () if rows is None else (*extra, rows)
    return ref.at[(*lead, *(fixed.get(d, slice(None)) for d in dims), *tail)]


def sum_kernel(g_hbm, t_ref, x_ref, gap_ref, acc, rows_ref, g, f_ref, turned1, turned2, landed, q,
               stage1, sums1, stage2, sums2, stage3, local_sem, *sems):
    turn_sems, core_sems, rs_sems, ag_sems, pair_sems = (sems[2 * i:2 * i + 2] for i in range(5))
    me = where()
    c = me["c"]
    twin = moved(me, "c", 1)
    peers = [twin] + [moved(me, a, k) for a in "xyz" for k in (1, 2, 3)]
    barrier = pltpu.get_barrier_semaphore()
    for peer in peers:
        pl.semaphore_signal(barrier, inc=1, device_id=device(peer), device_id_type=MESH)
    pl.semaphore_wait(barrier, len(peers))
    sent = []

    def part_rows(p):
        return pl.ds(p * ROWS, ROWS)

    def received(copies):
        for copy in copies:
            copy.wait_recv()

    turning, moves = {}, {}

    def turned(unit, step):
        kept, started = turning.pop((unit, step), (None, ()))
        if kept is not None:
            kept.wait()
        received(started)

    def turn(unit, step):
        axis, p, lo = TURN_ORDERS[unit % 3][step], unit // 2, unit % 2
        if step:
            turned(unit, step - 1)
        place = lambda spot: {axis: spot[axis] // 2 if axis == "z" else spot[axis]}
        whole = lambda ref, fixed: cut(ref, fixed, part_rows(p), extra=(lo,))
        between = lambda ref, fixed: cut(ref, fixed, lead=(unit,))
        source = lambda fixed: between((turned1, turned2)[step - 1], fixed) if step else whole(g_hbm, fixed)
        target = lambda fixed: whole(g, fixed) if step == 2 else between((turned1, turned2)[step], fixed)
        kept = pltpu.make_async_copy(source(place(me)), target(place(me)), local_sem.at[unit * 3 + step])
        kept.start()
        started = []
        for k in (2,) if axis == "z" else (2, 1, 3):
            peer = moved(me, axis, k)
            index = unit * 9 + step * 3 + k - 1
            started.append(send(source(place(peer)), target(place(me)), turn_sems, index, peer))
        sent.extend(started)
        turning[unit, step] = kept, started

    def product(p, y, column):
        left = g[y, :, :, :, part_rows(p)].reshape(16 * ROWS, 512)
        right = t_ref[:, pl.ds(pl.multiple_of(column * HALF, HALF), HALF)]
        return jnp.dot(left, right, preferred_element_type=F32).reshape(SIDE, SIDE, ROWS, HALF)

    pairs = {}

    def pair(p):
        turned(2 * p, 2)
        turned(2 * p + 1, 2)

        @pl.loop(0, SIDE)
        def _(y):
            q[p, y] = product(p, y, 1 - c).astype(BF16)

        pairs[p] = send(q.at[p], landed.at[p], core_sems, p, twin)

    def both(p):
        pairs[p].wait_send()
        pairs[p].wait_recv()

        @pl.loop(0, SIDE)
        def _(y):
            q[p, y] = (product(p, y, c) + landed[p, y].astype(F32)).astype(BF16)

        if p in AROUND:
            around(p)
        else:
            scatter(p, 0)

    sources, slots, totals = (q, sums1, sums2), (stage1, stage2, stage3), (sums1, sums2)

    def left_after(p, step):
        return "".join(d for d in "yxz" if d not in ORDERS[p][:step])

    def scatter(p, step):
        axis, moves[p] = ORDERS[p][step], []
        for k in (2, 1, 3):
            peer = moved(me, axis, k)
            source = cut(sources[step], {axis: peer[axis]}, lead=(p,), dims=left_after(p, step))
            moves[p].append(send(source, slots[step].at[p, k - 1], rs_sems, p * 10 + step * 3 + k - 1, peer))
        sent.extend(moves[p])

    def halfway(p, at, half):
        axis, across, _ = ORDERS[p][0], *left_after(p, 1)
        return cut(q, {axis: at[axis], across: pl.ds(2 * half, 2)}, lead=(p,))

    def around(p):
        axis = ORDERS[p][0]
        moves[p] = [
            send(halfway(p, moved(me, axis, 2), half), stage1.at[p, 1, pl.ds(2 * half, 2)], rs_sems,
                 p * 10 + (1, 9)[half], moved(me, axis, k))
            for half, k in enumerate((1, 3))
        ]
        sent.extend(moves[p])

    def onward(p):
        axis, passed, moves[p] = ORDERS[p][0], moves[p], []
        for half, k in enumerate((1, 3)):
            passed[half].wait_recv()
            peer = moved(me, axis, k)
            mine = halfway(p, peer, half)
            for i in (0, 1):
                mine[i] = (mine[i].astype(F32) + stage1[p, 1, 2 * half + i].astype(F32)).astype(BF16)
            source = cut(q, {axis: peer[axis]}, lead=(p,))
            moves[p].append(send(source, stage1.at[p, k - 1], rs_sems, p * 10 + k - 1, peer))
        sent.extend(moves[p])

    def add(p, step):
        axis = ORDERS[p][step]
        ways = (0, 2) if step == 0 and p in AROUND else (0, 1, 2)
        received(moves[p])
        mine = cut(sources[step], {axis: me[axis]}, lead=(p,), dims=left_after(p, step))

        def total(at):
            value = mine[(*at,)].astype(F32)
            for k in ways:
                value += slots[step][(p, k, *at)].astype(F32)
            return value

        if step == 0:
            @pl.loop(0, SIDE)
            def _(a):
                totals[0][p, a] = total((a,))
        elif step == 1:
            totals[1][p] = total((slice(None),))
        else:
            f_ref[c, me["y"], me["x"], me["z"], part_rows(p)] = total((slice(None),)).astype(BF16)
        if step < 2:
            scatter(p, step + 1)
        else:
            gather(p, 2)

    def gather(p, step):
        part = cut(f_ref, {a: me[a] for a in ORDERS[p][:step + 1]}, part_rows(p), (c,))
        ways = (1, 3) if step == 0 and p in PASSED else (2, 1, 3)
        moves[p] = [
            send(part, part, ag_sems, p * 10 + step * 3 + k - 1, moved(me, ORDERS[p][step], k)) for k in ways
        ]
        sent.extend(moves[p])

    def further(p, step):
        received(moves[p])
        gather(p, step)
        if step == 0:
            pairs[p] = []
            share(p, 0)

    def piece(p, k, half=None):
        axis, across, _ = ORDERS[p][0], *left_after(p, 1)
        fixed = {axis: lax.rem(me[axis] + SIDE - k, SIDE)}
        if half is not None:
            fixed[across] = pl.ds(2 * half, 2)
        return cut(f_ref, fixed, part_rows(p), (c,))

    def share(p, k):
        pairs[p].append(send(piece(p, k), piece(p, k), pair_sems, p * SIDE + k, twin))
        sent.append(pairs[p][-1])

    def forward(p):
        came, moves[p] = moves[p], []
        for half, k in enumerate((1, 3)):
            came[half].wait_recv()
            part = piece(p, k, half)
            moves[p].append(send(part, part, ag_sems, p * 10 + (1, 9)[half], moved(me, ORDERS[p][0], k)))
            share(p, k)
        sent.extend(moves[p])

    def share_rest(p):
        for copy, k in zip(moves[p], (2, 2) if p in PASSED else (2, 1, 3)):
            copy.wait_recv()
            if p not in PASSED:
                share(p, k)
        if p in PASSED:
            share(p, 2)

    def multiply(p):
        received(pairs[p])
        s = jnp.concatenate([f_ref[h, :, :, :, part_rows(p)].reshape(64 * ROWS, HALF) for h in (0, 1)], axis=1)
        w = g[:, :, :, :, part_rows(p)].reshape(64 * ROWS, 512)
        acc[...] += lax.dot_general(
            s, jnp.concatenate([s, w], axis=1), (((0,), (0,)), ((), ())), preferred_element_type=F32
        )

    acc[...] = jnp.zeros_like(acc)
    steps = {f.__name__: f for f in (turn, pair, both, onward, add, further, forward, share_rest, multiply)}
    for name, *args in PLAN:
        steps[name](*args)

    for h in (0, 1):
        for lo in (0, 1):
            rows_ref[h, pl.ds(lo * CHIP_ROWS, CHIP_ROWS)] = f_ref[h, me["y"], me["x"], me["z"] // 2 * 2 + lo]
    factor(acc, x_ref, gap_ref)
    for copy in sent:
        copy.wait_send()


def dot(u, v, across=False):
    return lax.dot_general(
        u.astype(BF16), v.astype(BF16), (((1,), (1 if across else 0,)), ((), ())), preferred_element_type=F32
    )


def halves(u):
    high = u.astype(BF16)
    return high, (u - high.astype(F32)).astype(BF16)


def factor(acc, x_ref, gap_ref):
    k = acc.shape[0]
    row = lax.broadcasted_iota(jnp.int32, (k, k), 0)
    col = lax.broadcasted_iota(jnp.int32, (k, k), 1)
    eye = (row == col).astype(F32)
    half_lower = jnp.where(row > col, 1.0, 0.5 * eye)

    def change(x, gap):
        phi = (gap * half_lower).astype(BF16)
        y = dot(phi, x)
        return y - dot(phi, y)

    gram = acc[:, :k] / 7168
    diagonal = gram * eye
    down = lax.rsqrt(jnp.sum(diagonal, axis=1, keepdims=True))
    across = lax.rsqrt(jnp.sum(diagonal, axis=0, keepdims=True))
    a = gram * down * across
    high, low = halves(a)
    phi = (a - eye) * half_lower
    x = (eye - (phi - dot(phi, phi))).astype(BF16)
    x = (x.astype(F32) - change(x, dot(dot(x, high), x, True) - eye)).astype(BF16)
    left, rest = halves(dot(x, high) + dot(x, low))
    gap = dot(left, x, True) + dot(rest, x, True) - eye
    gap_ref[0, 0] = jnp.sum(gap * gap)
    x_ref[...] = (x.astype(F32) - change(x, gap)) * across


def finish_kernel(x_ref, m_ref, rows_ref, basis_ref, c_ref):
    high, low = halves(x_ref[...])
    m, m_low = halves(m_ref[...])
    c_ref[...] = (dot(high, m) + (dot(high, m_low) + dot(low, m))).astype(BF16)
    rows = jnp.concatenate([rows_ref[0], rows_ref[1]], axis=1)
    basis_ref[...] = dot(rows, high, True) + dot(rows, low, True)


def local(gate_weights, test_blocks):
    weights = gate_weights.reshape(SIDE, SIDE, 2, 2, CHIP_ROWS, 512)
    n = len(ORDERS)
    slot = lambda step, kind, *lead: pltpu.VMEM((n, *lead, *(SIDE for _ in range(3 - step)), ROWS, HALF), kind)
    turning = pltpu.VMEM((2 * n, SIDE, SIDE, 2, ROWS, 512), BF16)
    scratch = [
        pltpu.VMEM((SIDE, SIDE, 2, 2, CHIP_ROWS, 512), BF16),
        pltpu.VMEM((2, SIDE, SIDE, SIDE, CHIP_ROWS, HALF), BF16),
        turning, turning, slot(0, BF16), slot(0, BF16),
        slot(1, BF16, 3), slot(1, F32), slot(2, F32, 3), slot(2, F32), slot(3, F32, 3),
        pltpu.SemaphoreType.DMA((6 * n,)),
    ]
    for size in (18, 1, 10, 10, 4):
        scratch += [pltpu.SemaphoreType.DMA((size * n,))] * 2
    vmem, smem, hbm = (pl.BlockSpec(memory_space=m) for m in (pltpu.VMEM, pltpu.SMEM, pl.ANY))
    x, gap, acc, rows = pl.pallas_call(
        sum_kernel,
        out_shape=(
            jax.ShapeDtypeStruct((512, 512), F32),
            jax.ShapeDtypeStruct((1, 1), F32),
            jax.ShapeDtypeStruct((512, 1024), F32),
            jax.ShapeDtypeStruct((2, 224, HALF), BF16),
        ),
        in_specs=[hbm, vmem],
        out_specs=(vmem, smem, vmem, vmem),
        scratch_shapes=scratch,
        compiler_params=pltpu.CompilerParams(collective_id=0, has_side_effects=True, vmem_limit_bytes=VMEM_LIMIT),
    )(weights, test_blocks[0])

    def quick():
        return pl.pallas_call(
            finish_kernel,
            grid=(1,),
            out_shape=(jax.ShapeDtypeStruct((224, 512), F32), jax.ShapeDtypeStruct((512, 512), BF16)),
            in_specs=[
                pl.BlockSpec((512, 512), lambda i: (0, 0)),
                pl.BlockSpec((512, 512), lambda i: (0, 1)),
                pl.BlockSpec((2, 224, HALF), lambda i: (0, 0, 0)),
            ],
            out_specs=(pl.BlockSpec((224, 512), lambda i: (0, 0)), pl.BlockSpec((512, 512), lambda i: (0, 0))),
            compiler_params=pltpu.CompilerParams(vmem_limit_bytes=32 << 20),
        )(x, acc, rows)

    def exact():
        lower = jnp.linalg.cholesky(acc[:, :512] / 7168)
        x = lax.linalg.triangular_solve(lower, jnp.eye(512, dtype=F32), left_side=True, lower=True)
        high = functools.partial(jnp.dot, precision=lax.Precision.HIGHEST)
        s = jnp.concatenate([rows[0], rows[1]], axis=1).astype(F32)
        return high(s, x.T), high(x, acc[:, 512:]).astype(BF16)

    basis, coefficients = lax.cond(gap[0, 0] < 0.1, quick, exact)
    return basis, coefficients[None]


def solution(mesh):
    placed = (P(None, "expert", "tensor"), P("expert", "tensor", None))
    return jax.shard_map(
        local,
        mesh=mesh,
        in_specs=placed,
        out_specs=(P("expert", None), P("expert", None, "tensor")),
        check_vma=False,
    )
```

time: 896 us -> 321 us (0.36)
  waiting for transfers between devices: 620 us -> 0 us
  Pallas kernels: 0 us -> 151 us
  blocking collectives: 97.1 us -> 0 us
  between operations: 16.6 us -> 2.51 us
  matrix products: 28 us -> 17 us
    psum x2 -> x0, waiting for transfers between devices: 499 us -> none  [the longest x1 329 us: local(): gram = lax.psum(local_gram, 'expert')]
    pallas_call x0 -> x1, Pallas kernels: none -> 151 us  [local(): pl.pallas_call(sum_kernel, out_shape=(jax.ShapeDtypeStruct((512, 512), F3...]
    all_gather x1 -> x0, waiting for transfers between devices: 121 us -> none  [local(): lax.all_gather(basis_half, 'expert', axis=0, tiled=True)]
    all_to_all x1 -> x0, blocking collectives: 97.1 us -> none  [local(): lax.all_to_all(gate_weights, 'expert', split_axis=0, concat_axis=1, tiled...]
    dot_general x3 -> x2, matrix products: 20.4 us -> 4.15 us  [exact(): return (high(s, x.T), high(x, acc[:, 512:]).astype(BF16))]
  transfers between devices with their start and end apart: 3 -> 0, of which waited for: 3 -> 0; matrix products, arithmetic and copies ran while one was open for 0% -> 0% of each run, Pallas kernels for 0% -> 0%
where the time goes in v2:
time: 321 us; the launch traced here: 317 us
  Pallas kernels  151 us (47%)
  other arithmetic  126 us (39%)
  local copies, waits for them, and re-layouts  17.4 us (5%)
  matrix products  17 us (5%)
    pallas_call x1, Pallas kernels, local(): pl.pallas_call(sum_kernel, out_shape=(jax.ShapeDtypeStruct((512, 512), F3...  151 us
    another operation x14, other arithmetic, exact(): lower = jnp.linalg.cholesky(acc[:, :512] / 7168)  83.2 us
    another operation x3, other arithmetic, exact(): lax.linalg.triangular_solve(lower, jnp.eye(512, dtype=F32), left_side=Tru...  40.4 us
    another operation x13, local copies, waits for them, and re-layouts  13.5 us
    another operation x6, matrix products, exact(): lower = jnp.linalg.cholesky(acc[:, :512] / 7168)  7.21 us

profile of v2, /device:TPU:1, one launch (start us, length us, event | category | flops | bytes accessed | tf_op | source)
XLA Modules:
  0.0 316.8 jit_solution(12179020477497333939)
XLA Ops:
  0.6 150.6 %shard_map.45 = (f32[512,512]{1,0:T(8,128)}, f32[1,1]{1,0:T(1,128)}, f32[512,1024]{1,0:T(8,128)}, bf16[2,224,256]{2,1,0:T(8,128)(2,1)S(1)}) custom-call(bf16[4,4,2,2,112,512]{5,4,3,2,1,0:T(8,128)(2,1)} %bitcast.58, bf16[512,512]{1,0:T(8,128)(2,1)} %bitcast.59), custom_call_target="tpu_custom_call" | custom-call | tf_op jit(solution)/shard_map/pallas_call | solution.py:334
  151.8 163.6 %conditional.1 = (f32[224,512]{1,0:T(8,128)}, bf16[1,512,512]{2,1,0:T(8,128)(2,1)}) conditional(s32[]{:T(128)} %bitcast.17, (bf16[2,224,256]{2,1,0:T(8,128)(2,1)S(1)}, f32[512,1024]{1,0:T(8,128)}) %tuple.17, (f32[512,512]{1,0:T(8,128)}, f32[512,1024]{1,0:T(8,128)}, bf16[2,224,256]{2,1,0:T(8,128)(2,1)S(1)}) %tuple.18), branch_computations={%region_0.9_spmd, %region_9.10_spmd} | conditional | flops 3730833920 | bytes 31363352 | solution.py:369
  151.8 2.1 copy.9
  153.9 1.1 slice_multiply_fusion
  155.0 1.6 copy.8
  156.6 1.2 fusion.2
  157.8 0.8 cholesky.100
  158.6 11.7 %cholesky.5 = f32[128,128]{1,0:T(8,128)S(1)} custom-call(f32[128,128]{1,0:T(8,128)S(1)} %cholesky.100), custom_call_target="Cholesky" | custom-call | tf_op jit(solution)/shard_map/cond/branch_0_fun/jit(cholesky)/cholesky | solution.py:363
  170.4 9.8 %custom-call.26 = f32[1,128,128]{1,2,0:T(8,128)S(1)} custom-call(f32[1,128,128]{2,1,0:T(8,128)S(1)} %get-tuple-element.63), custom_call_target="InvertDiagBlocksLowerTriangular" | custom-call | tf_op jit(solution)/shard_map/cond/branch_0_fun/jit(cholesky)/cholesky | solution.py:363
  180.2 0.1 cholesky.41
  180.3 1.2 constant_dynamic-update-slice_fusion.3
  181.6 1.3 convolution_subtract_fusion.3
  182.8 0.7 copy-done
  183.5 11.7 %cholesky.29 = f32[128,128]{1,0:T(8,128)S(1)} custom-call(f32[128,128]{1,0:T(8,128)S(1)} %cholesky.104), custom_call_target="Cholesky" | custom-call | tf_op jit(solution)/shard_map/cond/branch_0_fun/jit(cholesky)/cholesky | solution.py:363
  195.3 0.7 compare_reduce_fusion.2
  197.2 10.0 %custom-call.27 = f32[1,128,128]{1,2,0:T(8,128)S(1)} custom-call(f32[1,128,128]{2,1,0:T(8,128)S(1)} %get-tuple-element.60), custom_call_target="InvertDiagBlocksLowerTriangular" | custom-call | tf_op jit(solution)/shard_map/cond/branch_0_fun/jit(cholesky)/cholesky | solution.py:363
  207.2 1.2 convolution_dynamic-update-slice_fusion
  208.4 1.3 convolution_subtract_fusion.4
  209.7 0.6 cholesky.111
  210.3 13.2 %cholesky.62 = f32[128,128]{1,0:T(8,128)} custom-call(f32[128,128]{1,0:T(8,128)} %cholesky.111), custom_call_target="Cholesky" | custom-call | tf_op jit(solution)/shard_map/cond/branch_0_fun/jit(cholesky)/cholesky | solution.py:363
  223.5 1.5 select_reduce_fusion.1
  225.0 0.6 compare_reduce_fusion.1
  226.2 11.3 %custom-call.28 = f32[1,128,128]{1,2,0:T(8,128)} custom-call(f32[1,128,128]{2,1,0:T(8,128)} %get-tuple-element.57), custom_call_target="InvertDiagBlocksLowerTriangular" | custom-call | tf_op jit(solution)/shard_map/cond/branch_0_fun/jit(cholesky)/cholesky | solution.py:363
  237.5 1.0 convolution_dynamic-update-slice_fusion.1
  238.6 1.2 convolution_subtract_fusion.5
  239.8 11.7 %cholesky.89 = f32[128,128]{1,0:T(8,128)S(1)} custom-call(f32[128,128]{1,0:T(8,128)S(1)} %convolution_subtract_fusion.5), custom_call_target="Cholesky" | custom-call | tf_op jit(solution)/shard_map/cond/branch_0_fun/jit(cholesky)/cholesky | solution.py:363
  251.5 0.3 select_reduce_fusion
  251.8 0.6 compare_reduce_fusion
  253.1 1.1 select_select_fusion
  254.2 11.5 %while.1 = (s32[]{:T(128)}, f32[512,512]{1,0:T(8,128)}, s32[4,2]{0,1:T(2,128)S(1)}, f32[4,128,128]{2,1,0:T(8,128)S(1)}, s32[]{:T(128)}) while((s32[]{:T(128)}, f32[512,512]{1,0:T(8,128)}, s32[4,2]{0,1:T(2,128)S(1)}, f32[4,128,128]{2,1,0:T(8,128)S(1)}, s32[]{:T(128)}) %tuple.47), condition=%wide.while_cond, body=%wide.while_body.sunk | while | flops 2 | bytes 131181 | solution.py:364
  254.3 0.5 fusion.47
  254.8 2.3 bitcast_dynamic-update-slice_fusion.2
  257.2 0.5 fusion.47
  257.7 2.3 bitcast_dynamic-update-slice_fusion.2
  260.1 0.5 fusion.47
  260.6 2.3 bitcast_dynamic-update-slice_fusion.2
  263.0 0.5 fusion.47
  263.5 2.2 bitcast_dynamic-update-slice_fusion.2
  265.7 39.3 %custom-call.29 = f32[4,128,128]{1,2,0:T(8,128)S(1)} custom-call(f32[4,128,128]{2,1,0:T(8,128)S(1)} %get-tuple-element.39), custom_call_target="InvertDiagBlocksLowerTriangular" | custom-call | tf_op jit(solution)/shard_map/cond/branch_0_fun/triangular_solve | solution.py:364
  305.1 0.3 fusion.14
  305.6 1.2 convolution_subtract_fusion.1
  306.8 0.4 fusion.29
  307.2 1.3 convolution_subtract_fusion
  308.6 0.4 fusion.27
  309.0 1.6 convolution_subtract_fusion.2
  310.6 0.4 fusion.26
  311.0 2.7 fusion
  313.7 1.5 fusion.8
  (14 shorter events, 0.6 us)
Async XLA Ops:
  182.8 0.7 copy-start

commit v3 on v2

--- a/solution.py
+++ b/solution.py
@@ -12,30 +12,38 @@
 SIDE = 4
 CHIP_ROWS = 112
 HALF = 256
+LANES = 128
 VMEM_LIMIT = 62 << 20
 ROWS = 16
-ORDERS = ("xyz", "yzx", "zxy", "xyz", "yzx", "zxy", "xyz")
-AROUND = (0, 1, 5, 6)
-PASSED = (0, 1, 3, 4)
+ORDERS = ("xzy", "xyz", "yxz", "yzx", "xyz", "yxz", "zxy", "xyz", "zxy", "zyx", "zxy", "yxz", "zyx", "yxz")
+AROUND = (2, 3, 7, 8, 11, 12, 13)
+PASSED = (0, 1, 4, 5, 6, 10)
 TURN_ORDERS = ("xyz", "yzx", "zxy")
 PLAN = (
     ("turn", 0, 0), ("turn", 1, 0), ("turn", 2, 0), ("turn", 3, 0), ("turn", 4, 0), ("turn", 5, 0), ("turn", 6, 0),
-    ("turn", 7, 0), ("turn", 8, 0), ("turn", 9, 0), ("turn", 10, 0), ("turn", 11, 0), ("turn", 12, 0),
-    ("turn", 13, 0), ("turn", 1, 1), ("turn", 2, 1), ("turn", 0, 1), ("turn", 4, 1), ("turn", 5, 1), ("turn", 3, 1),
-    ("turn", 7, 1), ("turn", 8, 1), ("turn", 6, 1), ("turn", 10, 1), ("turn", 11, 1), ("turn", 9, 1), ("turn", 13, 1),
-    ("turn", 1, 2), ("turn", 12, 1), ("turn", 0, 2), ("turn", 4, 2), ("turn", 2, 2), ("turn", 3, 2), ("turn", 7, 2),
-    ("turn", 5, 2), ("turn", 6, 2), ("turn", 10, 2), ("turn", 8, 2), ("turn", 9, 2), ("turn", 13, 2), ("turn", 11, 2),
-    ("pair", 0), ("both", 0), ("turn", 12, 2), ("pair", 1), ("both", 1), ("pair", 2), ("pair", 3), ("both", 2),
-    ("both", 3), ("pair", 4), ("both", 4), ("pair", 5), ("pair", 6), ("onward", 0), ("onward", 1), ("both", 5),
-    ("both", 6), ("add", 2, 0), ("add", 3, 0), ("add", 4, 0), ("onward", 5), ("add", 0, 0), ("add", 1, 0),
-    ("onward", 6), ("add", 4, 1), ("add", 3, 1), ("add", 2, 1), ("add", 5, 0), ("add", 0, 1), ("add", 6, 0),
-    ("add", 2, 2), ("add", 4, 2), ("add", 1, 1), ("add", 3, 2), ("add", 0, 2), ("add", 5, 1), ("further", 4, 1),
-    ("further", 3, 1), ("add", 1, 2), ("add", 6, 1), ("further", 0, 1), ("further", 2, 1), ("add", 5, 2),
-    ("further", 1, 1), ("further", 4, 0), ("further", 3, 0), ("add", 6, 2), ("further", 2, 0), ("further", 0, 0),
-    ("further", 5, 1), ("further", 1, 0), ("further", 6, 1), ("forward", 4), ("forward", 3), ("forward", 1),
-    ("forward", 0), ("share_rest", 2), ("further", 6, 0), ("further", 5, 0), ("share_rest", 4), ("share_rest", 3),
-    ("share_rest", 1), ("share_rest", 0), ("multiply", 2), ("multiply", 3), ("multiply", 0), ("multiply", 1),
-    ("share_rest", 5), ("share_rest", 6), ("multiply", 4), ("multiply", 5), ("multiply", 6),
+    ("turn", 7, 0), ("turn", 8, 0), ("turn", 9, 0), ("turn", 10, 0), ("turn", 11, 0), ("turn", 12, 0), ("turn", 13, 0),
+    ("turn", 1, 1), ("turn", 2, 1), ("turn", 0, 1), ("turn", 4, 1), ("turn", 5, 1), ("turn", 3, 1), ("turn", 7, 1),
+    ("turn", 8, 1), ("turn", 6, 1), ("turn", 10, 1), ("turn", 11, 1), ("turn", 9, 1), ("turn", 13, 1), ("turn", 1, 2),
+    ("turn", 12, 1), ("turn", 0, 2), ("turn", 4, 2), ("turn", 2, 2), ("turn", 3, 2), ("turn", 7, 2), ("turn", 5, 2),
+    ("turn", 6, 2), ("turn", 10, 2), ("turn", 8, 2), ("turn", 9, 2), ("turn", 13, 2), ("turn", 11, 2), ("pair", 0),
+    ("turn", 12, 2), ("both", 0), ("pair", 1), ("both", 1), ("pair", 2), ("pair", 3), ("both", 2), ("both", 3),
+    ("pair", 4), ("both", 4), ("pair", 5), ("pair", 6), ("onward", 2), ("onward", 3), ("add", 0, 0), ("both", 5),
+    ("both", 6), ("add", 5, 0), ("add", 6, 0), ("onward", 8), ("add", 1, 0), ("add", 2, 0), ("add", 9, 0),
+    ("add", 3, 0), ("add", 0, 1), ("add", 4, 0), ("onward", 11), ("onward", 7), ("onward", 13), ("add", 5, 1),
+    ("add", 1, 1), ("add", 10, 0), ("onward", 12), ("add", 6, 1), ("add", 9, 1), ("add", 0, 2), ("add", 8, 0),
+    ("add", 2, 1), ("add", 4, 1), ("add", 3, 1), ("add", 5, 2), ("add", 7, 0), ("add", 1, 2), ("add", 11, 0),
+    ("add", 10, 1), ("add", 12, 0), ("add", 9, 2), ("add", 13, 0), ("add", 2, 2), ("add", 6, 2), ("further", 0, 1),
+    ("add", 4, 2), ("further", 5, 1), ("add", 8, 1), ("further", 1, 1), ("add", 3, 2), ("add", 7, 1), ("add", 10, 2),
+    ("add", 11, 1), ("further", 9, 1), ("further", 2, 1), ("further", 0, 0), ("further", 4, 1), ("add", 12, 1),
+    ("further", 6, 1), ("add", 13, 1), ("add", 8, 2), ("further", 5, 0), ("further", 3, 1), ("further", 1, 0),
+    ("add", 7, 2), ("further", 10, 1), ("add", 11, 2), ("further", 9, 0), ("further", 2, 0), ("further", 4, 0),
+    ("further", 8, 1), ("add", 13, 2), ("forward", 0), ("add", 12, 2), ("further", 3, 0), ("further", 7, 1),
+    ("further", 11, 1), ("further", 6, 0), ("forward", 5), ("forward", 1), ("further", 10, 0), ("share_rest", 9),
+    ("further", 13, 1), ("share_rest", 2), ("forward", 4), ("further", 8, 0), ("forward", 6), ("share_rest", 0),
+    ("further", 12, 1), ("further", 11, 0), ("share_rest", 3), ("forward", 10), ("share_rest", 1), ("further", 7, 0),
+    ("further", 13, 0), ("share_rest", 5), ("share_rest", 4), ("multiply", 0), ("further", 12, 0), ("multiply", 1),
+    ("share_rest", 8), ("share_rest", 6), ("multiply", 2), ("share_rest", 10), ("share_rest", 11), ("multiply", 4),
+    ("share_rest", 7), ("multiply", 5), ("share_rest", 13), ("share_rest", 12), ("multiply", 3), ("multiply", 6),
 )
 
 
@@ -66,9 +74,11 @@
     return ref.at[(*lead, *(fixed.get(d, slice(None)) for d in dims), *tail)]
 
 
-def sum_kernel(g_hbm, t_ref, x_ref, gap_ref, acc, rows_ref, g, f_ref, turned1, turned2, landed, q,
-               stage1, sums1, stage2, sums2, stage3, local_sem, *sems):
+def sum_kernel(g_hbm, t_hbm, x_ref, gap_ref, acc_hbm, rows_ref, t_ref, acc, g, f_ref, turned1, turned2, landed, q,
+               stage1, sums1, stage2, sums2, stage3, own_sem, local_sem, *sems):
     turn_sems, core_sems, rs_sems, ag_sems, pair_sems = (sems[2 * i:2 * i + 2] for i in range(5))
+    load = pltpu.make_async_copy(t_hbm, t_ref, own_sem.at[0])
+    load.start()
     me = where()
     c = me["c"]
     twin = moved(me, "c", 1)
@@ -99,10 +109,11 @@
         if step:
             turned(unit, step - 1)
         place = lambda spot: {axis: spot[axis] // 2 if axis == "z" else spot[axis]}
-        whole = lambda ref, fixed: cut(ref, fixed, part_rows(p), extra=(lo,))
         between = lambda ref, fixed: cut(ref, fixed, lead=(unit,))
-        source = lambda fixed: between((turned1, turned2)[step - 1], fixed) if step else whole(g_hbm, fixed)
-        target = lambda fixed: whole(g, fixed) if step == 2 else between((turned1, turned2)[step], fixed)
+        first = lambda fixed: cut(g_hbm, fixed, part_rows(p), extra=(lo,))
+        last = lambda fixed: cut(g, fixed, lead=(p,), extra=(lo,), rows=slice(None))
+        source = lambda fixed: between((turned1, turned2)[step - 1], fixed) if step else first(fixed)
+        target = lambda fixed: last(fixed) if step == 2 else between((turned1, turned2)[step], fixed)
         kept = pltpu.make_async_copy(source(place(me)), target(place(me)), local_sem.at[unit * 3 + step])
         kept.start()
         started = []
@@ -114,11 +125,11 @@
         turning[unit, step] = kept, started
 
     def product(p, y, column):
-        left = g[y, :, :, :, part_rows(p)].reshape(16 * ROWS, 512)
+        left = g[p, y].reshape(16 * ROWS, 512)
         right = t_ref[:, pl.ds(pl.multiple_of(column * HALF, HALF), HALF)]
         return jnp.dot(left, right, preferred_element_type=F32).reshape(SIDE, SIDE, ROWS, HALF)
 
-    pairs = {}
+    pairs, shares = {}, {}
 
     def pair(p):
         turned(2 * p, 2)
@@ -126,9 +137,12 @@
 
         @pl.loop(0, SIDE)
         def _(y):
-            q[p, y] = product(p, y, 1 - c).astype(BF16)
-
-        pairs[p] = send(q.at[p], landed.at[p], core_sems, p, twin)
+            value = product(p, y, 1 - c).astype(BF16)
+            for h in (0, 1):
+                q[2 * p + h, y] = value[..., h * LANES:(h + 1) * LANES]
+
+        units = pl.ds(2 * p, 2)
+        pairs[p] = send(q.at[units], landed.at[units], core_sems, p, twin)
 
     def both(p):
         pairs[p].wait_send()
@@ -136,12 +150,17 @@
 
         @pl.loop(0, SIDE)
         def _(y):
-            q[p, y] = (product(p, y, c) + landed[p, y].astype(F32)).astype(BF16)
-
-        if p in AROUND:
-            around(p)
-        else:
-            scatter(p, 0)
+            value = product(p, y, c)
+            for h in (0, 1):
+                unit = 2 * p + h
+                part = value[..., h * LANES:(h + 1) * LANES]
+                q[unit, y] = (part + landed[unit, y].astype(F32)).astype(BF16)
+
+        for unit in (2 * p, 2 * p + 1):
+            if unit in AROUND:
+                around(unit)
+            else:
+                scatter(unit, 0)
 
     sources, slots, totals = (q, sums1, sums2), (stage1, stage2, stage3), (sums1, sums2)
 
@@ -200,14 +219,14 @@
         elif step == 1:
             totals[1][p] = total((slice(None),))
         else:
-            f_ref[c, me["y"], me["x"], me["z"], part_rows(p)] = total((slice(None),)).astype(BF16)
+            f_ref[c, p, me["y"], me["x"], me["z"]] = total((slice(None),)).astype(BF16)
         if step < 2:
             scatter(p, step + 1)
         else:
             gather(p, 2)
 
     def gather(p, step):
-        part = cut(f_ref, {a: me[a] for a in ORDERS[p][:step + 1]}, part_rows(p), (c,))
+        part = cut(f_ref, {a: me[a] for a in ORDERS[p][:step + 1]}, lead=(c, p))
         ways = (1, 3) if step == 0 and p in PASSED else (2, 1, 3)
         moves[p] = [
             send(part, part, ag_sems, p * 10 + step * 3 + k - 1, moved(me, ORDERS[p][step], k)) for k in ways
@@ -218,7 +237,7 @@
         received(moves[p])
         gather(p, step)
         if step == 0:
-            pairs[p] = []
+            shares[p] = []
             share(p, 0)
 
     def piece(p, k, half=None):
@@ -226,11 +245,11 @@
         fixed = {axis: lax.rem(me[axis] + SIDE - k, SIDE)}
         if half is not None:
             fixed[across] = pl.ds(2 * half, 2)
-        return cut(f_ref, fixed, part_rows(p), (c,))
+        return cut(f_ref, fixed, lead=(c, p))
 
     def share(p, k):
-        pairs[p].append(send(piece(p, k), piece(p, k), pair_sems, p * SIDE + k, twin))
-        sent.append(pairs[p][-1])
+        shares[p].append(send(piece(p, k), piece(p, k), pair_sems, p * SIDE + k, twin))
+        sent.append(shares[p][-1])
 
     def forward(p):
         came, moves[p] = moves[p], []
@@ -250,22 +269,30 @@
             share(p, 2)
 
     def multiply(p):
-        received(pairs[p])
-        s = jnp.concatenate([f_ref[h, :, :, :, part_rows(p)].reshape(64 * ROWS, HALF) for h in (0, 1)], axis=1)
-        w = g[:, :, :, :, part_rows(p)].reshape(64 * ROWS, 512)
+        units = (2 * p, 2 * p + 1)
+        for unit in units:
+            received(shares[unit])
+        s = jnp.concatenate([f_ref[h, unit].reshape(64 * ROWS, LANES) for h in (0, 1) for unit in units], axis=1)
+        w = g[p].reshape(64 * ROWS, 512)
         acc[...] += lax.dot_general(
             s, jnp.concatenate([s, w], axis=1), (((0,), (0,)), ((), ())), preferred_element_type=F32
         )
 
     acc[...] = jnp.zeros_like(acc)
+    load.wait()
     steps = {f.__name__: f for f in (turn, pair, both, onward, add, further, forward, share_rest, multiply)}
     for name, *args in PLAN:
         steps[name](*args)
 
-    for h in (0, 1):
+    for core in (0, 1):
         for lo in (0, 1):
-            rows_ref[h, pl.ds(lo * CHIP_ROWS, CHIP_ROWS)] = f_ref[h, me["y"], me["x"], me["z"] // 2 * 2 + lo]
+            for unit in range(len(ORDERS)):
+                at, lanes = pl.ds(lo * CHIP_ROWS + unit // 2 * ROWS, ROWS), pl.ds(unit % 2 * LANES, LANES)
+                rows_ref[core, at, lanes] = f_ref[core, unit, me["y"], me["x"], me["z"] // 2 * 2 + lo]
+    store = pltpu.make_async_copy(acc, acc_hbm, own_sem.at[1])
+    store.start()
     factor(acc, x_ref, gap_ref)
+    store.wait()
     for copy in sent:
         copy.wait_send()
 
@@ -318,17 +345,20 @@
 
 def local(gate_weights, test_blocks):
     weights = gate_weights.reshape(SIDE, SIDE, 2, 2, CHIP_ROWS, 512)
-    n = len(ORDERS)
-    slot = lambda step, kind, *lead: pltpu.VMEM((n, *lead, *(SIDE for _ in range(3 - step)), ROWS, HALF), kind)
+    n = len(ORDERS) // 2
+    slot = lambda step, kind, *lead: pltpu.VMEM((2 * n, *lead, *(SIDE for _ in range(3 - step)), ROWS, LANES), kind)
     turning = pltpu.VMEM((2 * n, SIDE, SIDE, 2, ROWS, 512), BF16)
     scratch = [
-        pltpu.VMEM((SIDE, SIDE, 2, 2, CHIP_ROWS, 512), BF16),
-        pltpu.VMEM((2, SIDE, SIDE, SIDE, CHIP_ROWS, HALF), BF16),
+        pltpu.VMEM((512, 512), BF16),
+        pltpu.VMEM((512, 1024), F32),
+        pltpu.VMEM((n, SIDE, SIDE, 2, 2, ROWS, 512), BF16),
+        pltpu.VMEM((2, 2 * n, SIDE, SIDE, SIDE, ROWS, LANES), BF16),
         turning, turning, slot(0, BF16), slot(0, BF16),
         slot(1, BF16, 3), slot(1, F32), slot(2, F32, 3), slot(2, F32), slot(3, F32, 3),
+        pltpu.SemaphoreType.DMA((2,)),
         pltpu.SemaphoreType.DMA((6 * n,)),
     ]
-    for size in (18, 1, 10, 10, 4):
+    for size in (18, 1, 20, 20, 8):
         scratch += [pltpu.SemaphoreType.DMA((size * n,))] * 2
     vmem, smem, hbm = (pl.BlockSpec(memory_space=m) for m in (pltpu.VMEM, pltpu.SMEM, pl.ANY))
     x, gap, acc, rows = pl.pallas_call(
@@ -339,8 +369,8 @@
             jax.ShapeDtypeStruct((512, 1024), F32),
             jax.ShapeDtypeStruct((2, 224, HALF), BF16),
         ),
-        in_specs=[hbm, vmem],
-        out_specs=(vmem, smem, vmem, vmem),
+        in_specs=[hbm, hbm],
+        out_specs=(vmem, smem, hbm, vmem),
         scratch_shapes=scratch,
         compiler_params=pltpu.CompilerParams(collective_id=0, has_side_effects=True, vmem_limit_bytes=VMEM_LIMIT),
     )(weights, test_blocks[0])

time: 321 us -> 317 us (0.988)
  Pallas kernels: 151 us -> 147 us
    pallas_call x1, Pallas kernels: 151 us -> 147 us  [local(): pl.pallas_call(sum_kernel, out_shape=(jax.ShapeDtypeStruct((512, 512), F3...]
where the time goes in v3:
time: 317 us; the launch traced here: 313 us
  Pallas kernels  147 us (46%)
  other arithmetic  126 us (40%)
  local copies, waits for them, and re-layouts  17.4 us (5%)
  matrix products  17 us (5%)
    pallas_call x1, Pallas kernels, local(): pl.pallas_call(sum_kernel, out_shape=(jax.ShapeDtypeStruct((512, 512), F3...  147 us
    another operation x14, other arithmetic, exact(): lower = jnp.linalg.cholesky(acc[:, :512] / 7168)  83.3 us
    another operation x3, other arithmetic, exact(): lax.linalg.triangular_solve(lower, jnp.eye(512, dtype=F32), left_side=Tru...  40.4 us
    another operation x13, local copies, waits for them, and re-layouts  13.6 us
    another operation x6, matrix products, exact(): lower = jnp.linalg.cholesky(acc[:, :512] / 7168)  7.2 us

profile of v3, /device:TPU:1, one launch (start us, length us, event | category | flops | bytes accessed | tf_op | source)
XLA Modules:
  0.0 312.9 jit_solution(18215182001819661416)
XLA Ops:
  0.6 147.0 %shard_map.45 = (f32[512,512]{1,0:T(8,128)}, f32[1,1]{1,0:T(1,128)}, f32[512,1024]{1,0:T(8,128)}, bf16[2,224,256]{2,1,0:T(8,128)(2,1)S(1)}) custom-call(bf16[4,4,2,2,112,512]{5,4,3,2,1,0:T(8,128)(2,1)} %bitcast.58, bf16[512,512]{1,0:T(8,128)(2,1)} %bitcast.59), custom_call_target="tpu_custom_call" | custom-call | tf_op jit(solution)/shard_map/pallas_call | solution.py:364
  148.1 163.7 %conditional.1 = (f32[224,512]{1,0:T(8,128)}, bf16[1,512,512]{2,1,0:T(8,128)(2,1)}) conditional(s32[]{:T(128)} %bitcast.17, (bf16[2,224,256]{2,1,0:T(8,128)(2,1)S(1)}, f32[512,1024]{1,0:T(8,128)}) %tuple.17, (f32[512,512]{1,0:T(8,128)}, f32[512,1024]{1,0:T(8,128)}, bf16[2,224,256]{2,1,0:T(8,128)(2,1)S(1)}) %tuple.18), branch_computations={%region_0.9_spmd, %region_9.10_spmd} | conditional | flops 3730833920 | bytes 31363352 | solution.py:399
  148.2 2.1 copy.9
  150.3 1.1 slice_multiply_fusion
  151.4 1.6 copy.8
  153.0 1.2 fusion.2
  154.2 0.8 cholesky.100
  155.0 11.7 %cholesky.5 = f32[128,128]{1,0:T(8,128)S(1)} custom-call(f32[128,128]{1,0:T(8,128)S(1)} %cholesky.100), custom_call_target="Cholesky" | custom-call | tf_op jit(solution)/shard_map/cond/branch_0_fun/jit(cholesky)/cholesky | solution.py:393
  166.8 9.8 %custom-call.26 = f32[1,128,128]{1,2,0:T(8,128)S(1)} custom-call(f32[1,128,128]{2,1,0:T(8,128)S(1)} %get-tuple-element.63), custom_call_target="InvertDiagBlocksLowerTriangular" | custom-call | tf_op jit(solution)/shard_map/cond/branch_0_fun/jit(cholesky)/cholesky | solution.py:393
  176.6 0.1 cholesky.41
  176.7 1.2 constant_dynamic-update-slice_fusion.3
  178.0 1.3 convolution_subtract_fusion.3
  179.2 0.7 copy-done
  179.9 11.7 %cholesky.29 = f32[128,128]{1,0:T(8,128)S(1)} custom-call(f32[128,128]{1,0:T(8,128)S(1)} %cholesky.104), custom_call_target="Cholesky" | custom-call | tf_op jit(solution)/shard_map/cond/branch_0_fun/jit(cholesky)/cholesky | solution.py:393
  191.7 0.7 compare_reduce_fusion.2
  193.6 10.2 %custom-call.27 = f32[1,128,128]{1,2,0:T(8,128)S(1)} custom-call(f32[1,128,128]{2,1,0:T(8,128)S(1)} %get-tuple-element.60), custom_call_target="InvertDiagBlocksLowerTriangular" | custom-call | tf_op jit(solution)/shard_map/cond/branch_0_fun/jit(cholesky)/cholesky | solution.py:393
  203.8 1.2 convolution_dynamic-update-slice_fusion
  205.0 1.3 convolution_subtract_fusion.4
  206.2 0.6 cholesky.111
  206.9 13.2 %cholesky.62 = f32[128,128]{1,0:T(8,128)} custom-call(f32[128,128]{1,0:T(8,128)} %cholesky.111), custom_call_target="Cholesky" | custom-call | tf_op jit(solution)/shard_map/cond/branch_0_fun/jit(cholesky)/cholesky | solution.py:393
  220.1 1.5 select_reduce_fusion.1
  221.6 0.6 compare_reduce_fusion.1
  222.8 11.3 %custom-call.28 = f32[1,128,128]{1,2,0:T(8,128)} custom-call(f32[1,128,128]{2,1,0:T(8,128)} %get-tuple-element.57), custom_call_target="InvertDiagBlocksLowerTriangular" | custom-call | tf_op jit(solution)/shard_map/cond/branch_0_fun/jit(cholesky)/cholesky | solution.py:393
  234.1 1.0 convolution_dynamic-update-slice_fusion.1
  235.2 1.2 convolution_subtract_fusion.5
  236.4 11.7 %cholesky.89 = f32[128,128]{1,0:T(8,128)S(1)} custom-call(f32[128,128]{1,0:T(8,128)S(1)} %convolution_subtract_fusion.5), custom_call_target="Cholesky" | custom-call | tf_op jit(solution)/shard_map/cond/branch_0_fun/jit(cholesky)/cholesky | solution.py:393
  248.1 0.2 select_reduce_fusion
  248.3 0.6 compare_reduce_fusion
  249.6 1.1 select_select_fusion
  250.7 11.5 %while.1 = (s32[]{:T(128)}, f32[512,512]{1,0:T(8,128)}, s32[4,2]{0,1:T(2,128)S(1)}, f32[4,128,128]{2,1,0:T(8,128)S(1)}, s32[]{:T(128)}) while((s32[]{:T(128)}, f32[512,512]{1,0:T(8,128)}, s32[4,2]{0,1:T(2,128)S(1)}, f32[4,128,128]{2,1,0:T(8,128)S(1)}, s32[]{:T(128)}) %tuple.47), condition=%wide.while_cond, body=%wide.while_body.sunk | while | flops 2 | bytes 131181 | solution.py:394
  250.8 0.5 fusion.47
  251.4 2.3 bitcast_dynamic-update-slice_fusion.2
  253.7 0.5 fusion.47
  254.2 2.3 bitcast_dynamic-update-slice_fusion.2
  256.6 0.5 fusion.47
  257.1 2.3 bitcast_dynamic-update-slice_fusion.2
  259.5 0.5 fusion.47
  260.0 2.2 bitcast_dynamic-update-slice_fusion.2
  262.2 39.3 %custom-call.29 = f32[4,128,128]{1,2,0:T(8,128)S(1)} custom-call(f32[4,128,128]{2,1,0:T(8,128)S(1)} %get-tuple-element.39), custom_call_target="InvertDiagBlocksLowerTriangular" | custom-call | tf_op jit(solution)/shard_map/cond/branch_0_fun/triangular_solve | solution.py:394
  301.6 0.3 fusion.14
  302.1 1.2 convolution_subtract_fusion.1
  303.3 0.4 fusion.29
  303.7 1.3 convolution_subtract_fusion
  305.1 0.4 fusion.27
  305.5 1.6 convolution_subtract_fusion.2
  307.1 0.4 fusion.26
  307.5 2.7 fusion
  310.2 1.5 fusion.8
  (14 shorter events, 0.6 us)
Async XLA Ops:
  179.2 0.7 copy-start

commit v4 on v3

--- a/solution.py
+++ b/solution.py
@@ -310,37 +310,74 @@
 
 def factor(acc, x_ref, gap_ref):
     k = acc.shape[0]
-    row = lax.broadcasted_iota(jnp.int32, (k, k), 0)
-    col = lax.broadcasted_iota(jnp.int32, (k, k), 1)
-    eye = (row == col).astype(F32)
-    half_lower = jnp.where(row > col, 1.0, 0.5 * eye)
+    h = k // 2
+    spots = ((0, 0), (1, 0), (1, 1))
+    part = lambda u, i, j: u[i * h:(i + 1) * h, j * h:(j + 1) * h]
+    blocks = lambda f, *us: {at: f(*(u[at] for u in us)) for at in spots}
+    row = lax.broadcasted_iota(jnp.int32, (h, h), 0)
+    col = lax.broadcasted_iota(jnp.int32, (h, h), 1)
+    one = (row == col).astype(F32)
+    half = jnp.where(row > col, 1.0, 0.5 * one)
+    eye = {(0, 0): one, (1, 0): jnp.zeros_like(one), (1, 1): one}
+    half_lower = {(0, 0): half, (1, 0): jnp.ones_like(one), (1, 1): half}
+    minus = lambda u, v: u - v
+    times = lambda u, v: u * v
+    half_precise = lambda u: u.astype(BF16)
+
+    def lower_lower(u, v):
+        return {
+            (0, 0): dot(u[0, 0], v[0, 0]),
+            (1, 0): dot(u[1, 0], v[0, 0]) + dot(u[1, 1], v[1, 0]),
+            (1, 1): dot(u[1, 1], v[1, 1]),
+        }
+
+    def lower_whole(u, v):
+        return {
+            (0, 0): dot(u[0, 0], part(v, 0, 0)),
+            (1, 0): dot(u[1, 0], part(v, 0, 0)) + dot(u[1, 1], part(v, 1, 0)),
+            (1, 1): dot(u[1, 0], part(v, 0, 1)) + dot(u[1, 1], part(v, 1, 1)),
+        }
+
+    def lower_across(u, v):
+        return {
+            (0, 0): dot(u[0, 0], v[0, 0], True),
+            (1, 0): dot(u[1, 0], v[0, 0], True),
+            (1, 1): dot(u[1, 0], v[1, 0], True) + dot(u[1, 1], v[1, 1], True),
+        }
 
     def change(x, gap):
-        phi = (gap * half_lower).astype(BF16)
-        y = dot(phi, x)
-        return y - dot(phi, y)
+        phi = blocks(half_precise, blocks(times, gap, half_lower))
+        y = lower_lower(phi, x)
+        return blocks(minus, y, lower_lower(phi, y))
 
     gram = acc[:, :k] / 7168
-    diagonal = gram * eye
-    down = lax.rsqrt(jnp.sum(diagonal, axis=1, keepdims=True))
-    across = lax.rsqrt(jnp.sum(diagonal, axis=0, keepdims=True))
+    diagonals = [part(gram, i, i) * one for i in (0, 1)]
+    down = lax.rsqrt(jnp.concatenate([jnp.sum(d, axis=1, keepdims=True) for d in diagonals], axis=0))
+    across = lax.rsqrt(jnp.concatenate([jnp.sum(d, axis=0, keepdims=True) for d in diagonals], axis=1))
     a = gram * down * across
     high, low = halves(a)
-    phi = (a - eye) * half_lower
-    x = (eye - (phi - dot(phi, phi))).astype(BF16)
-    x = (x.astype(F32) - change(x, dot(dot(x, high), x, True) - eye)).astype(BF16)
-    left, rest = halves(dot(x, high) + dot(x, low))
-    gap = dot(left, x, True) + dot(rest, x, True) - eye
-    gap_ref[0, 0] = jnp.sum(gap * gap)
-    x_ref[...] = (x.astype(F32) - change(x, gap)) * across
+    phi = {at: (part(a, *at) - eye[at]) * half_lower[at] for at in spots}
+    x = blocks(half_precise, blocks(minus, eye, blocks(minus, phi, lower_lower(phi, phi))))
+    gap = blocks(minus, lower_across(lower_whole(x, high), x), eye)
+    x = blocks(half_precise, blocks(lambda u, v: u.astype(F32) - v, x, change(x, gap)))
+    both = blocks(halves, blocks(lambda u, v: u + v, lower_whole(x, high), lower_whole(x, low)))
+    left, rest = (blocks(lambda u: u[i], both) for i in (0, 1))
+    gap = blocks(lambda u, v, w: u + v - w, lower_across(left, x), lower_across(rest, x), eye)
+    gap_ref[0, 0] = sum(jnp.sum(gap[at] * gap[at] * (2.0 * half_lower[at])) for at in spots)
+    x = blocks(lambda u, v: u.astype(F32) - v, x, change(x, gap))
+    x_ref[:h, h:] = jnp.zeros((h, h), F32)
+    for i, j in spots:
+        x_ref[i * h:(i + 1) * h, j * h:(j + 1) * h] = x[i, j] * across[:, j * h:(j + 1) * h]
 
 
 def finish_kernel(x_ref, m_ref, rows_ref, basis_ref, c_ref):
-    high, low = halves(x_ref[...])
+    h = x_ref.shape[0] // 2
+    rows = jnp.concatenate([rows_ref[0], rows_ref[1]], axis=1)
     m, m_low = halves(m_ref[...])
-    c_ref[...] = (dot(high, m) + (dot(high, m_low) + dot(low, m))).astype(BF16)
-    rows = jnp.concatenate([rows_ref[0], rows_ref[1]], axis=1)
-    basis_ref[...] = dot(rows, high, True) + dot(rows, low, True)
+    for at, width in ((0, h), (h, 2 * h)):
+        high, low = halves(x_ref[at:at + h, :width])
+        c_ref[at:at + h] = (dot(high, m[:width]) + (dot(high, m_low[:width]) + dot(low, m[:width]))).astype(BF16)
+        basis_ref[:, at:at + h] = dot(rows[:, :width], high, True) + dot(rows[:, :width], low, True)
 
 
 def local(gate_weights, test_blocks):

time: 317 us -> 317 us (level)
  no operation moved by 1% of the time
where the time goes in v4:
time: 317 us; the launch traced here: 312 us
  Pallas kernels  146 us (46%)
  other arithmetic  126 us (40%)
  local copies, waits for them, and re-layouts  17.4 us (5%)
  matrix products  17 us (5%)
    pallas_call x1, Pallas kernels, local(): pl.pallas_call(sum_kernel, out_shape=(jax.ShapeDtypeStruct((512, 512), F3...  146 us
    another operation x14, other arithmetic, exact(): lower = jnp.linalg.cholesky(acc[:, :512] / 7168)  83.2 us
    another operation x3, other arithmetic, exact(): lax.linalg.triangular_solve(lower, jnp.eye(512, dtype=F32), left_side=Tru...  40.4 us
    another operation x13, local copies, waits for them, and re-layouts  13.5 us
    another operation x6, matrix products, exact(): lower = jnp.linalg.cholesky(acc[:, :512] / 7168)  7.2 us

profile of v4, /device:TPU:1, one launch (start us, length us, event | category | flops | bytes accessed | tf_op | source)
XLA Modules:
  0.0 312.4 jit_solution(12845962427869007298)
XLA Ops:
  0.6 146.3 %shard_map.45 = (f32[512,512]{1,0:T(8,128)}, f32[1,1]{1,0:T(1,128)}, f32[512,1024]{1,0:T(8,128)}, bf16[2,224,256]{2,1,0:T(8,128)(2,1)S(1)}) custom-call(bf16[4,4,2,2,112,512]{5,4,3,2,1,0:T(8,128)(2,1)} %bitcast.58, bf16[512,512]{1,0:T(8,128)(2,1)} %bitcast.59), custom_call_target="tpu_custom_call" | custom-call | tf_op jit(solution)/shard_map/pallas_call | solution.py:401
  147.5 163.6 %conditional.1 = (f32[224,512]{1,0:T(8,128)}, bf16[1,512,512]{2,1,0:T(8,128)(2,1)}) conditional(s32[]{:T(128)} %bitcast.17, (bf16[2,224,256]{2,1,0:T(8,128)(2,1)S(1)}, f32[512,1024]{1,0:T(8,128)}) %tuple.17, (f32[512,512]{1,0:T(8,128)}, f32[512,1024]{1,0:T(8,128)}, bf16[2,224,256]{2,1,0:T(8,128)(2,1)S(1)}) %tuple.18), branch_computations={%region_0.9_spmd, %region_9.10_spmd} | conditional | flops 3730833920 | bytes 31363352 | solution.py:436
  147.5 2.1 copy.9
  149.6 1.1 slice_multiply_fusion
  150.7 1.6 copy.8
  152.2 1.2 fusion.2
  153.4 0.8 cholesky.100
  154.3 11.7 %cholesky.5 = f32[128,128]{1,0:T(8,128)S(1)} custom-call(f32[128,128]{1,0:T(8,128)S(1)} %cholesky.100), custom_call_target="Cholesky" | custom-call | tf_op jit(solution)/shard_map/cond/branch_0_fun/jit(cholesky)/cholesky | solution.py:430
  166.0 9.8 %custom-call.26 = f32[1,128,128]{1,2,0:T(8,128)S(1)} custom-call(f32[1,128,128]{2,1,0:T(8,128)S(1)} %get-tuple-element.63), custom_call_target="InvertDiagBlocksLowerTriangular" | custom-call | tf_op jit(solution)/shard_map/cond/branch_0_fun/jit(cholesky)/cholesky | solution.py:430
  175.9 0.1 cholesky.41
  176.0 1.2 constant_dynamic-update-slice_fusion.3
  177.2 1.3 convolution_subtract_fusion.3
  178.5 0.7 copy-done
  179.2 11.7 %cholesky.29 = f32[128,128]{1,0:T(8,128)S(1)} custom-call(f32[128,128]{1,0:T(8,128)S(1)} %cholesky.104), custom_call_target="Cholesky" | custom-call | tf_op jit(solution)/shard_map/cond/branch_0_fun/jit(cholesky)/cholesky | solution.py:430
  190.9 0.7 compare_reduce_fusion.2
  192.9 10.0 %custom-call.27 = f32[1,128,128]{1,2,0:T(8,128)S(1)} custom-call(f32[1,128,128]{2,1,0:T(8,128)S(1)} %get-tuple-element.60), custom_call_target="InvertDiagBlocksLowerTriangular" | custom-call | tf_op jit(solution)/shard_map/cond/branch_0_fun/jit(cholesky)/cholesky | solution.py:430
  202.9 1.2 convolution_dynamic-update-slice_fusion
  204.0 1.3 convolution_subtract_fusion.4
  205.3 0.6 cholesky.111
  206.0 13.2 %cholesky.62 = f32[128,128]{1,0:T(8,128)} custom-call(f32[128,128]{1,0:T(8,128)} %cholesky.111), custom_call_target="Cholesky" | custom-call | tf_op jit(solution)/shard_map/cond/branch_0_fun/jit(cholesky)/cholesky | solution.py:430
  219.1 1.5 select_reduce_fusion.1
  220.6 0.6 compare_reduce_fusion.1
  221.9 11.3 %custom-call.28 = f32[1,128,128]{1,2,0:T(8,128)} custom-call(f32[1,128,128]{2,1,0:T(8,128)} %get-tuple-element.57), custom_call_target="InvertDiagBlocksLowerTriangular" | custom-call | tf_op jit(solution)/shard_map/cond/branch_0_fun/jit(cholesky)/cholesky | solution.py:430
  233.2 1.0 convolution_dynamic-update-slice_fusion.1
  234.2 1.2 convolution_subtract_fusion.5
  235.5 11.7 %cholesky.89 = f32[128,128]{1,0:T(8,128)S(1)} custom-call(f32[128,128]{1,0:T(8,128)S(1)} %convolution_subtract_fusion.5), custom_call_target="Cholesky" | custom-call | tf_op jit(solution)/shard_map/cond/branch_0_fun/jit(cholesky)/cholesky | solution.py:430
  247.2 0.3 select_reduce_fusion
  247.5 0.6 compare_reduce_fusion
  248.8 1.1 select_select_fusion
  249.9 11.5 %while.1 = (s32[]{:T(128)}, f32[512,512]{1,0:T(8,128)}, s32[4,2]{0,1:T(2,128)S(1)}, f32[4,128,128]{2,1,0:T(8,128)S(1)}, s32[]{:T(128)}) while((s32[]{:T(128)}, f32[512,512]{1,0:T(8,128)}, s32[4,2]{0,1:T(2,128)S(1)}, f32[4,128,128]{2,1,0:T(8,128)S(1)}, s32[]{:T(128)}) %tuple.47), condition=%wide.while_cond, body=%wide.while_body.sunk | while | flops 2 | bytes 131181 | solution.py:431
  250.0 0.5 fusion.47
  250.5 2.3 bitcast_dynamic-update-slice_fusion.2
  252.9 0.5 fusion.47
  253.4 2.3 bitcast_dynamic-update-slice_fusion.2
  255.8 0.5 fusion.47
  256.3 2.3 bitcast_dynamic-update-slice_fusion.2
  258.6 0.5 fusion.47
  259.2 2.2 bitcast_dynamic-update-slice_fusion.2
  261.4 39.3 %custom-call.29 = f32[4,128,128]{1,2,0:T(8,128)S(1)} custom-call(f32[4,128,128]{2,1,0:T(8,128)S(1)} %get-tuple-element.39), custom_call_target="InvertDiagBlocksLowerTriangular" | custom-call | tf_op jit(solution)/shard_map/cond/branch_0_fun/triangular_solve | solution.py:431
  300.8 0.3 fusion.14
  301.3 1.2 convolution_subtract_fusion.1
  302.5 0.4 fusion.29
  302.9 1.3 convolution_subtract_fusion
  304.2 0.4 fusion.27
  304.7 1.6 convolution_subtract_fusion.2
  306.2 0.4 fusion.26
  306.7 2.7 fusion
  309.3 1.5 fusion.8
  (14 shorter events, 0.6 us)
Async XLA Ops:
  178.5 0.7 copy-start

commit v5 on v4

--- a/solution.py
+++ b/solution.py
@@ -274,9 +274,13 @@
             received(shares[unit])
         s = jnp.concatenate([f_ref[h, unit].reshape(64 * ROWS, LANES) for h in (0, 1) for unit in units], axis=1)
         w = g[p].reshape(64 * ROWS, 512)
-        acc[...] += lax.dot_general(
-            s, jnp.concatenate([s, w], axis=1), (((0,), (0,)), ((), ())), preferred_element_type=F32
+        contract = functools.partial(
+            lax.dot_general, dimension_numbers=(((0,), (0,)), ((), ())), preferred_element_type=F32
         )
+        top = contract(s[:, :HALF], jnp.concatenate([s[:, :HALF], w], axis=1))
+        acc[:HALF, :HALF] += top[:, :HALF]
+        acc[:HALF, 2 * HALF:] += top[:, HALF:]
+        acc[HALF:] += contract(s[:, HALF:], jnp.concatenate([s, w], axis=1))
 
     acc[...] = jnp.zeros_like(acc)
     load.wait()
@@ -331,11 +335,11 @@
             (1, 1): dot(u[1, 1], v[1, 1]),
         }
 
-    def lower_whole(u, v):
+    def lower_symmetric(u, v):
         return {
             (0, 0): dot(u[0, 0], part(v, 0, 0)),
             (1, 0): dot(u[1, 0], part(v, 0, 0)) + dot(u[1, 1], part(v, 1, 0)),
-            (1, 1): dot(u[1, 0], part(v, 0, 1)) + dot(u[1, 1], part(v, 1, 1)),
+            (1, 1): dot(u[1, 0], part(v, 1, 0), True) + dot(u[1, 1], part(v, 1, 1)),
         }
 
     def lower_across(u, v):
@@ -358,9 +362,9 @@
     high, low = halves(a)
     phi = {at: (part(a, *at) - eye[at]) * half_lower[at] for at in spots}
     x = blocks(half_precise, blocks(minus, eye, blocks(minus, phi, lower_lower(phi, phi))))
-    gap = blocks(minus, lower_across(lower_whole(x, high), x), eye)
+    gap = blocks(minus, lower_across(lower_symmetric(x, high), x), eye)
     x = blocks(half_precise, blocks(lambda u, v: u.astype(F32) - v, x, change(x, gap)))
-    both = blocks(halves, blocks(lambda u, v: u + v, lower_whole(x, high), lower_whole(x, low)))
+    both = blocks(halves, blocks(lambda u, v: u + v, lower_symmetric(x, high), lower_symmetric(x, low)))
     left, rest = (blocks(lambda u: u[i], both) for i in (0, 1))
     gap = blocks(lambda u, v, w: u + v - w, lower_across(left, x), lower_across(rest, x), eye)
     gap_ref[0, 0] = sum(jnp.sum(gap[at] * gap[at] * (2.0 * half_lower[at])) for at in spots)
@@ -427,7 +431,7 @@
         )(x, acc, rows)
 
     def exact():
-        lower = jnp.linalg.cholesky(acc[:, :512] / 7168)
+        lower = jnp.linalg.cholesky(acc[:, :512] / 7168, symmetrize_input=False)
         x = lax.linalg.triangular_solve(lower, jnp.eye(512, dtype=F32), left_side=True, lower=True)
         high = functools.partial(jnp.dot, precision=lax.Precision.HIGHEST)
         s = jnp.concatenate([rows[0], rows[1]], axis=1).astype(F32)

time: 317 us -> 293 us (0.924)
  local copies, waits for them, and re-layouts: 17.4 us -> 8.03 us
  matrix products: 17 us -> 9.01 us
  other arithmetic: 126 us -> 120 us
    another operation x17 -> x16, local copies, waits for them, and re-layouts: 15.1 us -> 8.01 us
    another operation x6, matrix products: 7.2 us -> 1.88 us  [exact(): lower = jnp.linalg.cholesky(acc[:, :512] / 7168, symmetrize_input=False)]
    another operation x14, other arithmetic: 83.2 us -> 78.5 us  [exact(): lower = jnp.linalg.cholesky(acc[:, :512] / 7168, symmetrize_input=False)]
where the time goes in v5:
time: 293 us; the launch traced here: 289 us
  Pallas kernels  147 us (50%)
  other arithmetic  120 us (41%)
  matrix products  9.01 us (3%)
  local copies, waits for them, and re-layouts  8.03 us (3%)
  loops' own time  3.47 us (1%)
    pallas_call x1, Pallas kernels, local(): pl.pallas_call(sum_kernel, out_shape=(jax.ShapeDtypeStruct((512, 512), F3...  147 us
    another operation x14, other arithmetic, exact(): lower = jnp.linalg.cholesky(acc[:, :512] / 7168, symmetrize_input=False)  78.5 us
    another operation x3, other arithmetic, exact(): lax.linalg.triangular_solve(lower, jnp.eye(512, dtype=F32), left_side=Tru...  39.4 us
    another operation x12, local copies, waits for them, and re-layouts  7.87 us

profile of v5, /device:TPU:1, one launch (start us, length us, event | category | flops | bytes accessed | tf_op | source)
XLA Modules:
  0.0 289.4 jit_solution(5095487099847706135)
XLA Ops:
  0.6 146.8 %shard_map.45 = (f32[512,512]{1,0:T(8,128)S(1)}, f32[1,1]{1,0:T(1,128)}, f32[512,1024]{1,0:T(8,128)}, bf16[2,224,256]{2,1,0:T(8,128)(2,1)S(1)}) custom-call(bf16[4,4,2,2,112,512]{5,4,3,2,1,0:T(8,128)(2,1)} %bitcast.54, bf16[512,512]{1,0:T(8,128)(2,1)} %bitcast.55), custom_call_target="tpu_custom_call" | custom-call | tf_op jit(solution)/shard_map/pallas_call | solution.py:405
  148.0 140.0 %conditional.1 = (f32[224,512]{1,0:T(8,128)}, bf16[1,512,512]{2,1,0:T(8,128)(2,1)}) conditional(s32[]{:T(128)} %bitcast.16, (bf16[2,224,256]{2,1,0:T(8,128)(2,1)S(1)}, f32[512,1024]{1,0:T(8,128)}) %tuple.17, (f32[512,512]{1,0:T(8,128)S(1)}, f32[512,1024]{1,0:T(8,128)}, bf16[2,224,256]{2,1,0:T(8,128)(2,1)S(1)}) %tuple.18), branch_computations={%region_0.9_spmd, %region_9.10_spmd} | conditional | flops 3730047488 | bytes 29528348 | solution.py:440
  148.1 1.3 slice_multiply_fusion
  149.4 11.7 %cholesky.5 = f32[128,128]{1,0:T(8,128)S(1)} custom-call(f32[128,128]{1,0:T(8,128)S(1)} %cholesky.100), custom_call_target="Cholesky" | custom-call | tf_op jit(solution)/shard_map/cond/branch_0_fun/jit(cholesky)/cholesky | solution.py:434
  161.2 9.8 %custom-call.26 = f32[1,128,128]{1,2,0:T(8,128)S(1)} custom-call(f32[1,128,128]{2,1,0:T(8,128)S(1)} %get-tuple-element.61), custom_call_target="InvertDiagBlocksLowerTriangular" | custom-call | tf_op jit(solution)/shard_map/cond/branch_0_fun/jit(cholesky)/cholesky | solution.py:434
  171.0 0.1 cholesky.41
  171.1 0.3 constant_dynamic-update-slice_fusion.3
  171.4 0.3 convolution_subtract_fusion.3
  171.8 11.7 %cholesky.29 = f32[128,128]{1,0:T(8,128)S(1)} custom-call(f32[128,128]{1,0:T(8,128)S(1)} %cholesky.104), custom_call_target="Cholesky" | custom-call | tf_op jit(solution)/shard_map/cond/branch_0_fun/jit(cholesky)/cholesky | solution.py:434
  183.5 0.6 compare_reduce_fusion.2
  185.5 10.0 %custom-call.27 = f32[1,128,128]{1,2,0:T(8,128)S(1)} custom-call(f32[1,128,128]{2,1,0:T(8,128)S(1)} %get-tuple-element.58), custom_call_target="InvertDiagBlocksLowerTriangular" | custom-call | tf_op jit(solution)/shard_map/cond/branch_0_fun/jit(cholesky)/cholesky | solution.py:434
  195.5 0.3 convolution_dynamic-update-slice_fusion
  195.7 0.4 convolution_subtract_fusion.4
  196.1 11.7 %cholesky.62 = f32[128,128]{1,0:T(8,128)S(1)} custom-call(f32[128,128]{1,0:T(8,128)S(1)} %cholesky.111), custom_call_target="Cholesky" | custom-call | tf_op jit(solution)/shard_map/cond/branch_0_fun/jit(cholesky)/cholesky | solution.py:434
  207.9 0.6 compare_reduce_fusion.1
  209.2 9.8 %custom-call.28 = f32[1,128,128]{1,2,0:T(8,128)S(1)} custom-call(f32[1,128,128]{2,1,0:T(8,128)S(1)} %get-tuple-element.55), custom_call_target="InvertDiagBlocksLowerTriangular" | custom-call | tf_op jit(solution)/shard_map/cond/branch_0_fun/jit(cholesky)/cholesky | solution.py:434
  219.0 0.2 convolution_dynamic-update-slice_fusion.1
  219.2 0.4 convolution_subtract_fusion.5
  219.6 11.7 %cholesky.89 = f32[128,128]{1,0:T(8,128)S(1)} custom-call(f32[128,128]{1,0:T(8,128)S(1)} %convolution_subtract_fusion.5), custom_call_target="Cholesky" | custom-call | tf_op jit(solution)/shard_map/cond/branch_0_fun/jit(cholesky)/cholesky | solution.py:434
  231.3 0.6 compare_reduce_fusion
  232.6 0.1 select_select_fusion
  232.8 8.2 %while.1 = (s32[]{:T(128)}, f32[512,512]{1,0:T(8,128)S(1)}, s32[4,2]{0,1:T(2,128)S(1)}, f32[4,128,128]{2,1,0:T(8,128)S(1)}, s32[]{:T(128)}) while((s32[]{:T(128)}, f32[512,512]{1,0:T(8,128)S(1)}, s32[4,2]{0,1:T(2,128)S(1)}, f32[4,128,128]{2,1,0:T(8,128)S(1)}, s32[]{:T(128)}) %tuple.46), condition=%wide.while_cond, body=%wide.while_body.sunk | while | flops 2 | bytes 131181 | solution.py:435
  233.1 0.1 constant_dynamic-slice_fusion.2
  233.1 0.5 fusion.46
  233.7 1.3 bitcast_dynamic-update-slice_fusion.2
  235.1 0.1 constant_dynamic-slice_fusion.2
  235.1 0.5 fusion.46
  235.7 1.3 bitcast_dynamic-update-slice_fusion.2
  237.1 0.1 constant_dynamic-slice_fusion.2
  237.1 0.5 fusion.46
  237.7 1.3 bitcast_dynamic-update-slice_fusion.2
  239.0 0.1 constant_dynamic-slice_fusion.2
  239.1 0.5 fusion.46
  239.7 1.3 bitcast_dynamic-update-slice_fusion.2
  241.0 39.3 %custom-call.29 = f32[4,128,128]{1,2,0:T(8,128)S(1)} custom-call(f32[4,128,128]{2,1,0:T(8,128)S(1)} %get-tuple-element.39), custom_call_target="InvertDiagBlocksLowerTriangular" | custom-call | tf_op jit(solution)/shard_map/cond/branch_0_fun/triangular_solve | solution.py:435
  280.3 0.1 iota_compare_fusion
  280.4 0.3 fusion.13
  280.8 0.1 fusion.11
  280.9 0.4 convolution_subtract_fusion.1
  281.3 0.0 copy-start
  281.3 0.4 fusion.28
  281.7 0.4 convolution_subtract_fusion
  282.1 0.4 fusion.26
  282.6 0.6 convolution_subtract_fusion.2
  283.2 0.4 fusion.25
  283.6 0.0 copy-done
  283.6 2.6 fusion
  286.3 1.5 fusion.7
  (11 shorter events, 0.2 us)
Async XLA Ops:
  281.3 2.4 copy-start
